TPU v7x, 32 devices: a whole 2x2x4 slice. The times are simulated.
32 devices in a mesh: grp: 2 (over x), row: 4 (over y, core), col: 4 (over z).
Axes of the slice: x: 2, y: 2, z: 4, core: 2. Of those that a mesh axis runs over, the one named last changes fastest.
Arguments:
- tokens: bfloat16 [16384, 512], P(('grp', 'row'), 'col'), may hold values from -6 to 6
- cotangent: bfloat16 [16384, 512], P(('grp', 'row'), 'col'), may hold values from -6 to 6
- norm1_gain: bfloat16 [512], P('col'), may hold values from 0.5 to 1.5
- norm1_bias: bfloat16 [512], P('col'), may hold values from -1 to 1
- qkv_weight: bfloat16 [512, 1536], P('col', 'row'), may hold values from -0.25 to 0.25
- out_weight: bfloat16 [512, 512], P('row', 'col'), may hold values from -1.5 to 1.5
- gate1_weight: bfloat16 [512, 512], P('row', 'col'), may hold values from -0.25 to 0.25
- gate1_bias: bfloat16 [512], P('col'), may hold values from -2.5 to 2.5
- norm2_gain: bfloat16 [512], P('col'), may hold values from 0.5 to 1.5
- norm2_bias: bfloat16 [512], P('col'), may hold values from -1 to 1
- up_weight: bfloat16 [512, 2048], P('col', 'row'), may hold values from -0.25 to 0.25
- up_bias: bfloat16 [2048], P('row'), may hold values from -1.5 to 1.5
- down_weight: bfloat16 [2048, 512], P('row', 'col'), may hold values from -0.1875 to 0.1875
- down_bias: bfloat16 [512], P('col'), may hold values from -1.5 to 1.5
- gate2_weight: bfloat16 [2048, 512], P('row', 'col'), may hold values from -0.125 to 0.125
- gate2_bias: bfloat16 [512], P('col'), may hold values from -2.5 to 2.5
Outputs:
- output: bfloat16 [16384, 512], P(('grp', 'row'), 'col')
- input_grad: bfloat16 [16384, 512], P(('grp', 'row'), 'col')
- grad_norm1_gain: float32 [512], P('col')
- grad_norm1_bias: float32 [512], P('col')
- grad_qkv: float32 [512, 1536], P('col', 'row')
- grad_out: float32 [512, 512], P('row', 'col')
- grad_gate1: float32 [512, 512], P('row', 'col')
- grad_gate1_bias: float32 [512], P('col')
- grad_norm2_gain: float32 [512], P('col')
- grad_norm2_bias: float32 [512], P('col')
- grad_up: float32 [512, 2048], P('col', 'row')
- grad_up_bias: float32 [2048], P('row')
- grad_down: float32 [2048, 512], P('row', 'col')
- grad_down_bias: float32 [512], P('col')
- grad_gate2: float32 [2048, 512], P('row', 'col')
- grad_gate2_bias: float32 [512], P('col')
All inputs are finite; a program needn't handle non-finite values.
Results may differ from a plain program's by a relative error of at most 0.014.
Values may be sent and summed in bfloat16 or wider, within the bound.
A program may use at most 128 MiB of HBM per device.

v0:
```python
from functools import partial

import jax
import jax.numpy as jnp
from jax import lax
from jax.sharding import PartitionSpec as P

D = 512
HD = 64
PROMPT = 1024
CONT = 128
NCONT = 8
GTOK = 2048


NORM_EPSILON = 1e-05
MASKED_SCORE = -1e30


def rows_whole(values):
    return lax.all_gather(values, "row", axis=0, tiled=True)


def cols_whole(values):
    return lax.all_gather(values, "col", axis=0, tiled=True)


def swish_slope(values):
    sigma = jax.nn.sigmoid(values)
    return sigma * (1.0 + values * (1.0 - sigma))


def sum_cols(whole, product):
    rows_here = whole.shape[0] // lax.axis_size("col")

    def term(begin_row, row_count):
        return product(whole)

    return lax.psum_scatter(
        term(jnp.int32(0), rows_here * lax.axis_size("col")), "col", scatter_dimension=0, tiled=True
    )


def sum_rows(whole, product):
    rows_here = whole.shape[0] // lax.axis_size("row")

    def term(begin_row, row_count):
        return product(whole)

    return lax.psum_scatter(
        term(jnp.int32(0), rows_here * lax.axis_size("row")), "row", scatter_dimension=0, tiled=True
    )


def times_plain(left_side, right):
    return jnp.dot(left_side, right, preferred_element_type=jnp.float32)


def times_back(left_side, right):
    return lax.dot_general(
        left_side, right, (((1,), (1,)), ((), ())), preferred_element_type=jnp.float32
    )


def outer_rows(left_side, right_side):
    return lax.dot_general(
        left_side, right_side, (((0,), (0,)), ((), ())), preferred_element_type=jnp.float32
    )


def col_totals(first_sum, second_sum):
    return lax.psum((first_sum, second_sum), "col")


def norm_forward(residual, gain, shift):
    totals, squares = col_totals(jnp.sum(residual, axis=1), jnp.sum(residual * residual, axis=1))
    average = totals / D
    variance = squares / D - average * average
    inverse = lax.rsqrt(variance + NORM_EPSILON)
    standard = (residual - average[:, None]) * inverse[:, None]
    normed = standard * gain.astype(jnp.float32) + shift.astype(jnp.float32)
    return (normed, standard, inverse)


def norm_backward(grad_normed, standard, inverse, gain):
    grad_standard = grad_normed * gain.astype(jnp.float32)
    first_total, second_total = col_totals(
        jnp.sum(grad_standard, axis=1), jnp.sum(grad_standard * standard, axis=1)
    )
    grad_residual = inverse[:, None] * (
        grad_standard - first_total[:, None] / D - standard * (second_total[:, None] / D)
    )
    return (grad_residual, jnp.sum(grad_normed * standard, axis=0), jnp.sum(grad_normed, axis=0))


def place_cols(local_sum):
    full_vector = jnp.zeros((local_sum.shape[0] * lax.axis_size("col"),), jnp.float32)
    return lax.dynamic_update_slice_in_dim(
        full_vector, local_sum, lax.axis_index("col") * local_sum.shape[0], 0
    )


def place_rows(local_sum):
    full_vector = jnp.zeros((local_sum.shape[0] * lax.axis_size("row"),), jnp.float32)
    return lax.dynamic_update_slice_in_dim(
        full_vector, local_sum, lax.axis_index("row") * local_sum.shape[0], 0
    )


def own_cols(full_vector, width_here):
    return lax.dynamic_slice_in_dim(full_vector, lax.axis_index("col") * width_here, width_here, 0)


def own_rows(full_vector, width_here):
    return lax.dynamic_slice_in_dim(full_vector, lax.axis_index("row") * width_here, width_here, 0)


def split_heads(qkv_rows):
    groups = qkv_rows.shape[0] // GTOK
    heads_here = qkv_rows.shape[1] // (3 * HD)
    shaped = qkv_rows.reshape(groups, GTOK, heads_here, 3, HD)
    return (shaped[:, :, :, 0], shaped[:, :, :, 1], shaped[:, :, :, 2])


def prompt_scores(block_queries, key_rows, block_index):
    query_count = block_queries.shape[1]
    raw_scores = jnp.einsum(
        "gqhe,gkhe->ghqk", block_queries, key_rows, preferred_element_type=jnp.float32
    ) * HD ** (-0.5)
    query_pos = block_index * query_count + lax.broadcasted_iota(
        jnp.int32, (query_count, key_rows.shape[1]), 0
    )
    key_pos = lax.broadcasted_iota(jnp.int32, (query_count, key_rows.shape[1]), 1)
    return jnp.where(key_pos <= query_pos, raw_scores, MASKED_SCORE)


def tail_scores(tail_queries, prompt_keys, tail_keys):
    shared = jnp.einsum(
        "gnqhe,gkhe->ghnqk", tail_queries, prompt_keys, preferred_element_type=jnp.float32
    ) * HD ** (-0.5)
    own_scores = jnp.einsum(
        "gnqhe,gnkhe->ghnqk", tail_queries, tail_keys, preferred_element_type=jnp.float32
    ) * HD ** (-0.5)
    query_pos = lax.broadcasted_iota(jnp.int32, (CONT, CONT), 0)
    key_pos = lax.broadcasted_iota(jnp.int32, (CONT, CONT), 1)
    return (shared, jnp.where(key_pos <= query_pos, own_scores, MASKED_SCORE))


def tail_split(whole_rows):
    groups, heads_here = (whole_rows.shape[0], whole_rows.shape[2])
    return whole_rows[:, PROMPT:].reshape(groups, NCONT, CONT, heads_here, HD)


def attend(qkv_rows):
    queries, key_rows, values = split_heads(qkv_rows)
    groups, heads_here = (queries.shape[0], queries.shape[2])
    block_rows = min(512, PROMPT)
    outputs = []
    prompt_lse = []
    for block_index in range(PROMPT // block_rows):
        block_end = (block_index + 1) * block_rows
        scores = prompt_scores(
            queries[:, block_index * block_rows : block_end], key_rows[:, :block_end], block_index
        )
        highest = jnp.max(scores, axis=-1, keepdims=True)
        weights = jnp.exp(scores - highest)
        row_total = jnp.sum(weights, axis=-1, keepdims=True)
        softmax_rows = (weights / row_total).astype(jnp.bfloat16)
        outputs.append(
            jnp.einsum(
                "ghqk,gkhe->gqhe",
                softmax_rows,
                values[:, :block_end],
                preferred_element_type=jnp.float32,
            )
        )
        prompt_lse.append(highest[..., 0] + jnp.log(row_total[..., 0]))
    tail_queries = tail_split(queries)
    shared, own_scores = tail_scores(tail_queries, key_rows[:, :PROMPT], tail_split(key_rows))
    highest = jnp.maximum(jnp.max(shared, axis=-1), jnp.max(own_scores, axis=-1))[..., None]
    shared_weights = jnp.exp(shared - highest)
    own_weights = jnp.exp(own_scores - highest)
    row_total = jnp.sum(shared_weights, axis=-1, keepdims=True) + jnp.sum(
        own_weights, axis=-1, keepdims=True
    )
    tail_out = jnp.einsum(
        "ghnqk,gkhe->gnqhe",
        (shared_weights / row_total).astype(jnp.bfloat16),
        values[:, :PROMPT],
        preferred_element_type=jnp.float32,
    )
    tail_out = tail_out + jnp.einsum(
        "ghnqk,gnkhe->gnqhe",
        (own_weights / row_total).astype(jnp.bfloat16),
        tail_split(values),
        preferred_element_type=jnp.float32,
    )
    outputs.append(tail_out.reshape(groups, NCONT * CONT, heads_here, HD))
    attended = (
        jnp.concatenate(outputs, axis=1)
        .reshape(groups * GTOK, heads_here * HD)
        .astype(jnp.bfloat16)
    )
    tail_lse = highest[..., 0] + jnp.log(row_total[..., 0])
    return (attended, jnp.concatenate(prompt_lse, axis=2), tail_lse)


def attend_back(qkv_rows, prompt_lse, tail_lse, grad_attended):
    queries, key_rows, values = split_heads(qkv_rows)
    groups, heads_here = (queries.shape[0], queries.shape[2])
    scale_factor = HD ** (-0.5)
    grad_rows = grad_attended.reshape(groups, GTOK, heads_here, HD)
    grad_keys = jnp.zeros((groups, GTOK, heads_here, HD), jnp.float32)
    grad_values = jnp.zeros((groups, GTOK, heads_here, HD), jnp.float32)
    grad_queries = []
    block_rows = min(512, PROMPT)
    for block_index in range(PROMPT // block_rows):
        block_start = block_index * block_rows
        block_end = block_start + block_rows
        block_queries = queries[:, block_start:block_end]
        scores = prompt_scores(block_queries, key_rows[:, :block_end], block_index)
        weights = jnp.exp(scores - prompt_lse[:, :, block_start:block_end, None])
        block_grad = grad_rows[:, block_start:block_end]
        grad_values = grad_values.at[:, :block_end].add(
            jnp.einsum(
                "ghqk,gqhe->gkhe",
                weights.astype(jnp.bfloat16),
                block_grad,
                preferred_element_type=jnp.float32,
            )
        )
        grad_weights = jnp.einsum(
            "gqhe,gkhe->ghqk", block_grad, values[:, :block_end], preferred_element_type=jnp.float32
        )
        row_inner = jnp.sum(weights * grad_weights, axis=-1, keepdims=True)
        grad_scores = (weights * (grad_weights - row_inner)).astype(jnp.bfloat16)
        grad_queries.append(
            jnp.einsum(
                "ghqk,gkhe->gqhe",
                grad_scores,
                key_rows[:, :block_end],
                preferred_element_type=jnp.float32,
            )
            * scale_factor
        )
        grad_keys = grad_keys.at[:, :block_end].add(
            jnp.einsum(
                "ghqk,gqhe->gkhe", grad_scores, block_queries, preferred_element_type=jnp.float32
            )
            * scale_factor
        )
    tail_queries = tail_split(queries)
    tail_keys = tail_split(key_rows)
    tail_values = tail_split(values)
    shared, own_scores = tail_scores(tail_queries, key_rows[:, :PROMPT], tail_keys)
    shared_weights = jnp.exp(shared - tail_lse[..., None])
    own_weights = jnp.exp(own_scores - tail_lse[..., None])
    tail_grad = tail_split(grad_rows)
    grad_shared = jnp.einsum(
        "gnqhe,gkhe->ghnqk", tail_grad, values[:, :PROMPT], preferred_element_type=jnp.float32
    )
    grad_own = jnp.einsum(
        "gnqhe,gnkhe->ghnqk", tail_grad, tail_values, preferred_element_type=jnp.float32
    )
    row_inner = jnp.sum(shared_weights * grad_shared, axis=-1, keepdims=True) + jnp.sum(
        own_weights * grad_own, axis=-1, keepdims=True
    )
    shared_scores = (shared_weights * (grad_shared - row_inner)).astype(jnp.bfloat16)
    own_grad_scores = (own_weights * (grad_own - row_inner)).astype(jnp.bfloat16)
    tail_query_grad = jnp.einsum(
        "ghnqk,gkhe->gnqhe", shared_scores, key_rows[:, :PROMPT], preferred_element_type=jnp.float32
    )
    tail_query_grad = tail_query_grad + jnp.einsum(
        "ghnqk,gnkhe->gnqhe", own_grad_scores, tail_keys, preferred_element_type=jnp.float32
    )
    grad_queries.append(
        tail_query_grad.reshape(groups, NCONT * CONT, heads_here, HD) * scale_factor
    )
    grad_keys = grad_keys.at[:, :PROMPT].add(
        jnp.einsum(
            "ghnqk,gnqhe->gkhe", shared_scores, tail_queries, preferred_element_type=jnp.float32
        )
        * scale_factor
    )
    tail_key_grad = (
        jnp.einsum(
            "ghnqk,gnqhe->gnkhe", own_grad_scores, tail_queries, preferred_element_type=jnp.float32
        )
        * scale_factor
    )
    grad_keys = grad_keys.at[:, PROMPT:].add(
        tail_key_grad.reshape(groups, NCONT * CONT, heads_here, HD)
    )
    grad_values = grad_values.at[:, :PROMPT].add(
        jnp.einsum(
            "ghnqk,gnqhe->gkhe",
            shared_weights.astype(jnp.bfloat16),
            tail_grad,
            preferred_element_type=jnp.float32,
        )
    )
    tail_value_grad = jnp.einsum(
        "ghnqk,gnqhe->gnkhe",
        own_weights.astype(jnp.bfloat16),
        tail_grad,
        preferred_element_type=jnp.float32,
    )
    grad_values = grad_values.at[:, PROMPT:].add(
        tail_value_grad.reshape(groups, NCONT * CONT, heads_here, HD)
    )
    stacked = jnp.stack([jnp.concatenate(grad_queries, axis=1), grad_keys, grad_values], axis=3)
    return stacked.reshape(groups * GTOK, heads_here * 3 * HD).astype(jnp.bfloat16)


def body(
    tokens,
    cotangent,
    norm1_gain,
    norm1_bias,
    qkv_weight,
    out_weight,
    gate1_weight,
    gate1_bias,
    norm2_gain,
    norm2_bias,
    up_weight,
    up_bias,
    down_weight,
    down_bias,
    gate2_weight,
    gate2_bias,
):
    col_width = tokens.shape[1]
    out_gate = jnp.concatenate([out_weight, gate1_weight], axis=1)
    residual = tokens.astype(jnp.float32)
    normed_one, standard_one, inverse_one = norm_forward(residual, norm1_gain, norm1_bias)
    whole_one = rows_whole(normed_one.astype(jnp.bfloat16))
    qkv_rows = sum_cols(whole_one, partial(times_plain, right=qkv_weight)).astype(jnp.bfloat16)
    attended, prompt_lse, tail_lse = attend(qkv_rows)
    attended_whole = cols_whole(attended)
    branch_one = sum_rows(attended_whole, partial(times_plain, right=out_gate))
    attn_out = branch_one[:, :col_width]
    gate_one = jax.nn.sigmoid(branch_one[:, col_width:] + gate1_bias.astype(jnp.float32))
    middle = residual + gate_one * attn_out
    normed_two, standard_two, inverse_two = norm_forward(middle, norm2_gain, norm2_bias)
    normed_low = normed_two.astype(jnp.bfloat16)
    down_gate = jnp.concatenate([down_weight, gate2_weight], axis=1)
    whole_two = rows_whole(normed_low)
    pre_up = sum_cols(whole_two, partial(times_plain, right=up_weight)) + up_bias.astype(
        jnp.float32
    )
    hidden = jax.nn.silu(pre_up).astype(jnp.bfloat16)
    hidden_whole = cols_whole(hidden)
    branch_two = sum_rows(hidden_whole, partial(times_plain, right=down_gate))
    ffn_pre, gate_pre = (branch_two[:, :col_width], branch_two[:, col_width:])
    ffn_out = ffn_pre + down_bias.astype(jnp.float32)
    gate_two = jax.nn.sigmoid(gate_pre + gate2_bias.astype(jnp.float32))
    output = (middle + gate_two * ffn_out).astype(jnp.bfloat16)
    grad_result = cotangent.astype(jnp.float32)
    grad_ffn = (grad_result * gate_two).astype(jnp.bfloat16)
    grad_gate_two = (grad_result * ffn_out * gate_two * (1.0 - gate_two)).astype(jnp.bfloat16)
    down_bias_sum = place_cols(jnp.sum(grad_ffn, axis=0, dtype=jnp.float32))
    gate2_bias_sum = place_cols(jnp.sum(grad_gate_two, axis=0, dtype=jnp.float32))
    pair_whole = rows_whole(jnp.concatenate([grad_ffn, grad_gate_two], axis=1))
    grad_pair_w = outer_rows(hidden_whole, pair_whole)
    grad_hidden = sum_cols(pair_whole, partial(times_back, right=down_gate))
    grad_up_rows = (grad_hidden * swish_slope(pre_up)).astype(jnp.bfloat16)
    up_bias_sum = place_rows(jnp.sum(grad_up_rows, axis=0, dtype=jnp.float32))
    grad_up_whole = cols_whole(grad_up_rows)
    grad_up_w = outer_rows(whole_two, grad_up_whole)
    grad_normed_two = sum_rows(grad_up_whole, partial(times_back, right=up_weight))
    grad_middle_norm, gain_two_sum, shift_two_sum = norm_backward(
        grad_normed_two, standard_two, inverse_two, norm2_gain
    )
    grad_middle = grad_result + grad_middle_norm
    grad_attn = (grad_middle * gate_one).astype(jnp.bfloat16)
    grad_gate_one = (grad_middle * attn_out * gate_one * (1.0 - gate_one)).astype(jnp.bfloat16)
    gate1_bias_sum = place_cols(jnp.sum(grad_gate_one, axis=0, dtype=jnp.float32))
    pair_one_whole = rows_whole(jnp.concatenate([grad_attn, grad_gate_one], axis=1))
    grad_out_gate = outer_rows(attended_whole, pair_one_whole)
    grad_attended = sum_cols(pair_one_whole, partial(times_back, right=out_gate)).astype(
        jnp.bfloat16
    )
    grad_qkv_rows = attend_back(qkv_rows, prompt_lse, tail_lse, grad_attended)
    grad_qkv_whole = cols_whole(grad_qkv_rows)
    grad_qkv_w = outer_rows(whole_one, grad_qkv_whole)
    grad_normed_one = sum_rows(grad_qkv_whole, partial(times_back, right=qkv_weight))
    grad_input_norm, gain_one_sum, shift_one_sum = norm_backward(
        grad_normed_one, standard_one, inverse_one, norm1_gain
    )
    input_grad = (grad_middle + grad_input_norm).astype(jnp.bfloat16)
    summed_qkv, summed_out_gate, summed_up, summed_pair = (
        lax.psum(grad_qkv_w.astype(jnp.bfloat16), "grp").astype(jnp.float32),
        lax.psum(grad_out_gate.astype(jnp.bfloat16), "grp").astype(jnp.float32),
        lax.psum(grad_up_w.astype(jnp.bfloat16), "grp").astype(jnp.float32),
        lax.psum(grad_pair_w.astype(jnp.bfloat16), "grp").astype(jnp.float32),
    )
    small_sums = lax.psum(
        (
            place_cols(gain_one_sum),
            place_cols(shift_one_sum),
            place_cols(gain_two_sum),
            place_cols(shift_two_sum),
            gate1_bias_sum,
            down_bias_sum,
            gate2_bias_sum,
            up_bias_sum,
        ),
        ("grp", "row", "col"),
    )
    return (
        output,
        input_grad,
        own_cols(small_sums[0], col_width),
        own_cols(small_sums[1], col_width),
        summed_qkv,
        summed_out_gate[:, :col_width],
        summed_out_gate[:, col_width:],
        own_cols(small_sums[4], col_width),
        own_cols(small_sums[2], col_width),
        own_cols(small_sums[3], col_width),
        summed_up,
        own_rows(small_sums[7], up_bias.shape[0]),
        summed_pair[:, :col_width],
        own_cols(small_sums[5], col_width),
        summed_pair[:, col_width:],
        own_cols(small_sums[6], col_width),
    )


def solution(mesh):
    return jax.shard_map(
        body,
        mesh=mesh,
        in_specs=(
            P(("grp", "row"), "col"),
            P(("grp", "row"), "col"),
            P("col"),
            P("col"),
            P("col", "row"),
            P("row", "col"),
            P("row", "col"),
            P("col"),
            P("col"),
            P("col"),
            P("col", "row"),
            P("row"),
            P("row", "col"),
            P("col"),
            P("row", "col"),
            P("col"),
        ),
        out_specs=(
            P(("grp", "row"), "col"),
            P(("grp", "row"), "col"),
            P("col"),
            P("col"),
            P("col", "row"),
            P("row", "col"),
            P("row", "col"),
            P("col"),
            P("col"),
            P("col"),
            P("col", "row"),
            P("row"),
            P("row", "col"),
            P("col"),
            P("row", "col"),
            P("col"),
        ),
        check_vma=False,
    )
```

profile of v0, /device:TPU:0, one launch (start us, length us, event | category | flops | bytes accessed | tf_op | source)
XLA Modules:
  0.0 1969.7 jit_solution(2649682921063279036)
XLA Ops:
  10.1 20.5 %all-reduce.6 = (f32[2048]{0:T(1024)S(1)}, f32[2048]{0:T(1024)S(1)}) all-reduce(f32[2048]{0:T(1024)S(1)} %get-tuple-element.123, f32[2048]{0:T(1024)S(1)} %get-tuple-element.122), channel_id=1, replica_groups=mesh['grp'=2,'row'=4,'col'=4] {'col'}, use_global_device_ids=true, to_apply=%region_3.0 | all-reduce | flops 4096 | bytes 32768 | tf_op jit(solution)/shard_map/psum | solution.py:72
  33.8 20.9 %all-gather.9.cloned.1.call-done = bf16[8192,128]{1,0:T(8,128)(2,1)} async-done(((bf16[2048,128]{1,0:T(8,128)(2,1)}), bf16[8192,128]{1,0:T(8,128)(2,1)}) %all-gather.9.cloned.1.call-update) | async-done | bytes 2097168 | tf_op jit(solution)/shard_map/all_gather | solution.py:21
  64.8 209.8 %reduce-scatter.9.cloned.1.call-done = f32[2048,384]{1,0:T(8,128)} async-done(((f32[8192,384]{1,0:T(8,128)}), f32[2048,384]{1,0:T(8,128)}) %reduce-scatter.9.cloned.1.call-update) | async-done | bytes 3145744 | tf_op jit(solution)/shard_map/reduce_scatter | solution.py:39
  293.1 47.0 %all-gather.11.cloned.1.call-done = bf16[8192,128]{0,1:T(8,128)(2,1)} async-done(((bf16[2048,128]{0,1:T(8,128)(2,1)}), bf16[8192,128]{0,1:T(8,128)(2,1)}) %all-gather.11.cloned.1.call-update) | async-done | bytes 2097168 | tf_op jit(solution)/shard_map/all_gather | solution.py:25
  348.4 68.4 %reduce-scatter.11.cloned.1.call-done = f32[2048,256]{1,0:T(8,128)} async-done(((f32[8192,256]{1,0:T(8,128)}), f32[2048,256]{1,0:T(8,128)}) %reduce-scatter.11.cloned.1.call-update) | async-done | bytes 2097168 | tf_op jit(solution)/shard_map/reduce_scatter | solution.py:50
  419.8 19.8 %all-reduce.5 = (f32[2048]{0:T(1024)}, f32[2048]{0:T(1024)}) all-reduce(f32[2048]{0:T(1024)} %get-tuple-element.121, f32[2048]{0:T(1024)S(1)} %get-tuple-element.120), channel_id=1, replica_groups=mesh['grp'=2,'row'=4,'col'=4] {'col'}, use_global_device_ids=true, to_apply=%region_17.18 | all-reduce | flops 4096 | bytes 32768 | tf_op jit(solution)/shard_map/psum | solution.py:72
  443.1 19.9 %all-gather.13.cloned.1.call-done = bf16[8192,128]{1,0:T(8,128)(2,1)} async-done(((bf16[2048,128]{1,0:T(8,128)(2,1)}), bf16[8192,128]{1,0:T(8,128)(2,1)}) %all-gather.13.cloned.1.call-update) | async-done | bytes 2097168 | tf_op jit(solution)/shard_map/all_gather | solution.py:21
  463.0 9.6 fusion.132
  474.0 279.1 %reduce-scatter.13.cloned.1.call-done = f32[2048,512]{1,0:T(8,128)} async-done(((f32[8192,512]{1,0:T(8,128)}), f32[2048,512]{1,0:T(8,128)}) %reduce-scatter.13.cloned.1.call-update) | async-done | bytes 4194320 | tf_op jit(solution)/shard_map/reduce_scatter | solution.py:39
  760.9 147.3 %all-gather.15.cloned.1.call-done = bf16[8192,512]{1,0:T(8,128)(2,1)} async-done(((bf16[2048,512]{1,0:T(8,128)(2,1)}), bf16[8192,512]{1,0:T(8,128)(2,1)}) %all-gather.15.cloned.1.call-update) | async-done | bytes 8388624 | tf_op jit(solution)/shard_map/all_gather | solution.py:25
  919.7 67.7 %reduce-scatter.15.cloned.1.call-done = f32[2048,256]{1,0:T(8,128)} async-done(((f32[8192,256]{1,0:T(8,128)}), f32[2048,256]{1,0:T(8,128)}) %reduce-scatter.15.cloned.1.call-update) | async-done | bytes 2097168 | tf_op jit(solution)/shard_map/reduce_scatter | solution.py:50
  992.3 34.6 %all-gather.17.cloned.1.call-done = bf16[8192,256]{1,0:T(8,128)(2,1)} async-done(((bf16[2048,256]{1,0:T(8,128)(2,1)}), bf16[8192,256]{1,0:T(8,128)(2,1)}) %all-gather.17.cloned.1.call-update) | async-done | bytes 4194320 | tf_op jit(solution)/shard_map/all_gather | solution.py:21
  1026.9 10.3 fusion.134
  1037.3 280.4 %reduce-scatter.17.cloned.1.call-done = f32[2048,512]{1,0:T(8,128)} async-done(((f32[8192,512]{1,0:T(8,128)}), f32[2048,512]{1,0:T(8,128)}) %reduce-scatter.17.cloned.1.call-update) | async-done | bytes 4194320 | tf_op jit(solution)/shard_map/reduce_scatter | solution.py:39
  1323.6 150.5 %all-gather.19.cloned.1.call-done = bf16[8192,512]{1,0:T(8,128)(2,1)} async-done(((bf16[2048,512]{1,0:T(8,128)(2,1)}), bf16[8192,512]{1,0:T(8,128)(2,1)}) %all-gather.19.cloned.1.call-update) | async-done | bytes 8388624 | tf_op jit(solution)/shard_map/all_gather | solution.py:25
  1481.9 42.8 %reduce-scatter.19.cloned.1.call-done = f32[2048,128]{1,0:T(8,128)} async-done(((f32[8192,128]{1,0:T(8,128)}), f32[2048,128]{1,0:T(8,128)}) %reduce-scatter.19.cloned.1.call-update) | async-done | bytes 1048592 | tf_op jit(solution)/shard_map/reduce_scatter | solution.py:50
  1527.6 18.7 all-reduce.4
  1552.7 31.8 %all-gather.21.cloned.1.call-done = bf16[8192,256]{1,0:T(8,128)(2,1)} async-done(((bf16[2048,256]{1,0:T(8,128)(2,1)}), bf16[8192,256]{1,0:T(8,128)(2,1)}) %all-gather.21.cloned.1.call-update) | async-done | bytes 4194320 | tf_op jit(solution)/shard_map/all_gather | solution.py:21
  1590.7 76.2 %reduce-scatter.21.cloned.1.call-done = f32[2048,128]{1,0:T(8,128)} async-done(((f32[8192,128]{1,0:T(8,128)}), f32[2048,128]{1,0:T(8,128)}) %reduce-scatter.21.cloned.1.call-update) | async-done | bytes 1048592 | tf_op jit(solution)/shard_map/reduce_scatter | solution.py:39
  1713.4 100.3 %all-gather.23.cloned.1.call-done = bf16[8192,384]{0,1:T(8,128)(2,1)} async-done(((bf16[2048,384]{0,1:T(8,128)(2,1)}), bf16[8192,384]{0,1:T(8,128)(2,1)}) %all-gather.23.cloned.1.call-update) | async-done | bytes 6291472 | tf_op jit(solution)/shard_map/all_gather | solution.py:25
  1827.8 19.5 all-reduce.10.cloned.1.call-done
  1853.8 40.5 %reduce-scatter.23.cloned.1.call-done = f32[2048,128]{1,0:T(8,128)} async-done(((f32[8192,128]{1,0:T(8,128)}), f32[2048,128]{1,0:T(8,128)}) %reduce-scatter.23.cloned.1.call-update) | async-done | bytes 1048592 | tf_op jit(solution)/shard_map/reduce_scatter | solution.py:50
  1897.1 39.6 %all-reduce.2 = (f32[512]{0:T(512)S(1)}, f32[512]{0:T(512)S(1)}, f32[512]{0:T(512)S(1)}, f32[512]{0:T(512)S(1)}, f32[512]{0:T(512)S(1)}, /*index=5*/f32[2048]{0:T(1024)S(1)}, f32[512]{0:T(512)S(1)}, f32[512]{0:T(512)S(1)}) all-reduce(f32[512]{0:T(512)S(1)} %dynamic_update_slice.24, ...), channel_id=1, replica_groups=mesh['grp'=2,'row'=4,'col'=4] {'grp','row','col'}, use_global_device_ids=true, to_apply=%region_37.38 | all-reduce | flops 5632 | bytes 45056 | tf_op jit(solution)/shard_map/psum | solution.py:398
  1941.5 17.6 all-reduce.3
  (307 shorter events, 181.2 us)
Async XLA Ops:
  7.2 455.8 %copy-start = (bf16[128,512]{1,0:T(8,128)(2,1)S(1)}, bf16[128,512]{1,0:T(8,128)(2,1)}, u32[]{:S(2)}) copy-start(bf16[128,512]{1,0:T(8,128)(2,1)} %param.42) | copy-start | bytes 393220
  7.2 47.5 %all-gather.9.cloned.1.call-start = ((), (), s32[]{:S(2)}) async-start(), calls=%async_computation.8 | async-start | bytes 2621440 | tf_op jit(solution)/shard_map/all_gather | solution.py:21
  33.7 240.9 %reduce-scatter.9.cloned.1.call-start = ((), (), s32[]{:S(2)}) async-start(), calls=%async_computation.9 | async-start | bytes 15728640 | tf_op jit(solution)/shard_map/reduce_scatter | solution.py:39
  62.6 277.5 %all-gather.11.cloned.1.call-start = ((), (), s32[]{:S(2)}) async-start(), calls=%async_computation.10 | async-start | bytes 2621440 | tf_op jit(solution)/shard_map/all_gather | solution.py:25
  292.9 123.9 %reduce-scatter.11.cloned.1.call-start = ((), (), s32[]{:S(2)}) async-start(), calls=%async_computation.11 | async-start | bytes 10485760 | tf_op jit(solution)/shard_map/reduce_scatter | solution.py:50
  346.3 116.7 %all-gather.13.cloned.1.call-start = ((), (), s32[]{:S(2)}) async-start(), calls=%async_computation.12 | async-start | bytes 2621440 | tf_op jit(solution)/shard_map/all_gather | solution.py:21
  443.0 310.1 %reduce-scatter.13.cloned.1.call-start = ((), (), s32[]{:S(2)}) async-start(), calls=%async_computation.13 | async-start | bytes 20971520 | tf_op jit(solution)/shard_map/reduce_scatter | solution.py:39
  472.7 435.6 %all-gather.15.cloned.1.call-start = ((), (), s32[]{:S(2)}) async-start(), calls=%async_computation.14 | async-start | bytes 10485760 | tf_op jit(solution)/shard_map/all_gather | solution.py:25
  757.7 229.7 %reduce-scatter.15.cloned.1.call-start = ((), (), s32[]{:S(2)}) async-start(), calls=%async_computation.15 | async-start | bytes 10485760 | tf_op jit(solution)/shard_map/reduce_scatter | solution.py:50
  917.3 109.6 %all-gather.17.cloned.1.call-start = ((), (), s32[]{:S(2)}) async-start(), calls=%async_computation.16 | async-start | bytes 5242880 | tf_op jit(solution)/shard_map/all_gather | solution.py:21
  992.2 325.4 %reduce-scatter.17.cloned.1.call-start = ((), (), s32[]{:S(2)}) async-start(), calls=%async_computation.17 | async-start | bytes 20971520 | tf_op jit(solution)/shard_map/reduce_scatter | solution.py:39
  1037.2 436.9 %all-gather.19.cloned.1.call-start = ((), (), s32[]{:S(2)}) async-start(), calls=%async_computation.18 | async-start | bytes 10485760 | tf_op jit(solution)/shard_map/all_gather | solution.py:25
  1323.6 201.2 %reduce-scatter.19.cloned.1.call-start = ((), (), s32[]{:S(2)}) async-start(), calls=%async_computation.19 | async-start | bytes 5242880 | tf_op jit(solution)/shard_map/reduce_scatter | solution.py:50
  1481.9 102.7 %all-gather.21.cloned.1.call-start = ((), (), s32[]{:S(2)}) async-start(), calls=%async_computation.20 | async-start | bytes 5242880 | tf_op jit(solution)/shard_map/all_gather | solution.py:21
  1552.7 114.3 %reduce-scatter.21.cloned.1.call-start = ((), (), s32[]{:S(2)}) async-start(), calls=%async_computation.21 | async-start | bytes 5242880 | tf_op jit(solution)/shard_map/reduce_scatter | solution.py:39
  1590.0 81.5 %copy-start.19 = (bf16[1,2048,2,64]{1,3,2,0:T(8,128)(2,1)S(1)}, bf16[1,2048,2,64]{1,3,2,0:T(8,128)(2,1)}, u32[]{:S(2)}) copy-start(bf16[1,2048,2,64]{1,3,2,0:T(8,128)(2,1)} %copy-done.18) | copy-start | bytes 1572868
  1590.0 223.7 %all-gather.23.cloned.1.call-start = ((), (), s32[]{:S(2)}) async-start(), calls=%async_computation.22 | async-start | bytes 7864320 | tf_op jit(solution)/shard_map/all_gather | solution.py:25
  1697.7 149.7 %all-reduce.10.cloned.1.call-start = ((), (), s32[]{:S(2)}) async-start(), calls=%async_computation.24 | async-start | bytes 1114112 | tf_op jit(solution)/shard_map/psum | solution.py:393
  1712.1 101.7 %copy-start.10 = (bf16[8192,128]{1,0:T(8,128)(2,1)S(1)}, bf16[8192,128]{1,0:T(8,128)(2,1)}, u32[]{:S(2)}) copy-start(bf16[8192,128]{1,0:T(8,128)(2,1)} %all-gather.9.cloned.1.call-done) | copy-start | bytes 6291460
  1713.4 105.8 %copy-start.34 = (bf16[128,384]{1,0:T(8,128)(2,1)S(1)}, bf16[128,384]{1,0:T(8,128)(2,1)}, u32[]{:S(2)}) copy-start(bf16[128,384]{1,0:T(8,128)(2,1)} %param.36) | copy-start | bytes 294916
  1819.2 75.1 %reduce-scatter.23.cloned.1.call-start = ((), (), s32[]{:S(2)}) async-start(), calls=%async_computation.23 | async-start | bytes 5242880 | tf_op jit(solution)/shard_map/reduce_scatter | solution.py:50
  1825.8 68.5 %copy-start.8 = (bf16[2048,128]{1,0:T(8,128)(2,1)S(1)}, bf16[2048,128]{1,0:T(8,128)(2,1)}, u32[]{:S(2)}) copy-start(bf16[2048,128]{1,0:T(8,128)(2,1)} %param.32) | copy-start | bytes 1572868
  1825.9 133.3 %copy-start.14 = (f32[2048,128]{1,0:T(8,128)S(1)}, f32[2048,128]{1,0:T(8,128)}, u32[]{:S(2)}) copy-start(f32[2048,128]{1,0:T(8,128)} %copy-done.13) | copy-start | bytes 3145732
  1825.9 137.0 %copy-start.1 = (bf16[128,512]{1,0:T(8,128)(2,1)S(1)}, bf16[128,512]{1,0:T(8,128)(2,1)}, u32[]{:S(2)}) copy-start(bf16[128,512]{1,0:T(8,128)(2,1)} %param.42) | copy-start | bytes 393220
  (60 other events, 638.6 us)
Sparse Core Ops, SparseCore 0:
  33.8 20.7 all-gather.8
  62.7 211.8 reduce-scatter.8
  293.1 46.9 all-gather.10
  346.4 70.4 reduce-scatter.10
  443.1 19.8 all-gather.12
  472.8 280.2 reduce-scatter.12
  757.8 150.3 all-gather.14
  917.4 69.9 reduce-scatter.14
  992.3 34.4 all-gather.16
  1037.3 280.2 reduce-scatter.16
  1323.7 150.3 all-gather.18
  1482.0 42.7 reduce-scatter.18
  1552.8 31.7 all-gather.20
  1590.2 76.7 reduce-scatter.20
  1697.8 115.8 all-gather.22
  1819.3 28.0 all-reduce.9
  1849.8 44.5 reduce-scatter.22
where the time goes:
time: 1970 us
  waiting for transfers between devices  1640 us (83%)
  blocking collectives  116 us (6%)
  matrix products  109 us (6%)
  other arithmetic  64.7 us (3%)
  local copies, waits for them, and re-layouts  25.9 us (1%)
    reduce_scatter x4, waiting for transfers between devices, sum_cols(): lax.psum_scatter(term(jnp.int32(0), rows_here * lax.axis_size('col')), 'c...  846 us
    all_gather x4, waiting for transfers between devices, cols_whole(): return lax.all_gather(values, 'col', axis=0, tiled=True)  445 us
    reduce_scatter x4, waiting for transfers between devices, sum_rows(): lax.psum_scatter(term(jnp.int32(0), rows_here * lax.axis_size('row')), 'r...  219 us
    all_gather x4, waiting for transfers between devices, rows_whole(): return lax.all_gather(values, 'row', axis=0, tiled=True)  107 us
    psum x4, blocking collectives, col_totals(): return lax.psum((first_sum, second_sum), 'col')  76.6 us
    psum x1, blocking collectives, body(): lax.psum((place_cols(gain_one_sum), place_cols(shift_one_sum), place_cols...  39.6 us
  transfers between devices with their start and end apart: 17, of which 17 were waited for; matrix products, arithmetic and copies ran while one was open for 2% of the time, Pallas kernels for 0%

commit v1 on v0

v1 whole, which is shorter than its diff:
```python
from functools import partial

import jax
import jax.numpy as jnp
from jax import lax
from jax.experimental import pallas as pl
from jax.experimental.pallas import tpu as pltpu
from jax.sharding import PartitionSpec as P

bf16 = jnp.bfloat16
f32 = jnp.float32
EPS = 1e-05
MASKED = -1e30
MESH = pl.DeviceIdType.MESH

T = 512
D = 512
BLOCK = {"qkv": (128, 384), "og": (128, 256), "up": (128, 512), "dg": (512, 256)}
NAMES = ("qkv", "og", "up", "dg")


def dot(a, b, ca, cb):
    return lax.dot_general(a, b, (((ca,), (cb,)), ((), ())), preferred_element_type=f32)


def loop(count, step):
    lax.fori_loop(0, count, lambda i, z: (step(i), z)[1], 0)


def cat(parts, axis=1):
    return jnp.concatenate(parts, axis=axis)


def sigmoid(v):
    return 1.0 / (1.0 + jnp.exp(-v))


def kernel(use_x, names_in, names_out, names_scr, *refs):
    ref = dict(zip(names_in + names_out + names_scr, refs))
    R = type("R", (), ref)
    a = lax.axis_index("grp")
    r = lax.axis_index("row")
    c = lax.axis_index("col")
    y, k = r // 2, r % 2
    ah = a % 2
    q = 2 * (c % 2) + k
    core = (a, 2 * y + 1 - k, c)
    yside = (a, 2 * (1 - y) + k, c)
    xside = (a + 1 - 2 * ah, r, c)
    zside = (a, r, c + 1 - 2 * (c % 2))
    owner_row = 2 * y + c // 2
    lo_row = pl.multiple_of(q * 128, 128)
    hi_row = pl.multiple_of((7 - q) * 128, 128)

    counter = [0]
    pending = []

    def send(src, dst, dev):
        i = counter[0]
        counter[0] += 1
        cp = pltpu.make_async_remote_copy(
            src_ref=src, dst_ref=dst, send_sem=R.ssem.at[i], recv_sem=R.rsem.at[i],
            device_id=dev, device_id_type=MESH)
        cp.start()
        pending.append(cp)
        return cp

    local = []

    def fetch(src, dst):
        cp = pltpu.make_async_copy(src, dst, R.lsem.at[len(local)])
        cp.start()
        local.append(cp)

    fetch(R.i_qkv, R.qstage)
    for t in range(2):
        for name, sources in (("og", ("out", "gate1")), ("up", ("up",)), ("dg", ("down", "gate2"))):
            rows, cols = BLOCK[name]
            rq = rows // 4
            w = getattr(R, "w_" + name)
            width = cols // len(sources)
            for j, s in enumerate(sources):
                at = pl.multiple_of((2 * t + ah) * rq, 32)
                fetch(getattr(R, "i_" + s).at[pl.ds(at, rq), :],
                      w.at[y, k, c, t, ah, :, pl.ds(j * width, width)])

    barrier = pltpu.get_barrier_semaphore()
    friends = [(a, 2 * y + kk, cc) for kk in range(2) for cc in range(4)]
    for kk in range(2):
        for cc in range(4):
            me = (k == kk) & (c == cc)

            @pl.when(jnp.logical_not(me))
            def _():
                pl.semaphore_signal(barrier, inc=1, device_id=(a, 2 * y + kk, cc), device_id_type=MESH)
    diag = (a, 2 * (1 - y) + 1 - k, c)
    for dev in (yside, xside, diag):
        pl.semaphore_signal(barrier, inc=1, device_id=dev, device_id_type=MESH)

    local[0].wait()
    for t in range(2):
        blk = R.qstage[pl.ds(pl.multiple_of((2 * t + ah) * 32, 32), 32), :].astype(f32)
        parts = [blk[:, (3 * h + j) * 64:(3 * h + j + 1) * 64] for j in range(3) for h in range(2)]
        R.w_qkv[y, k, c, t, ah] = cat(parts).astype(bf16)
    pl.semaphore_wait(barrier, 10)

    def rows_in(src, dst, which):
        sends = []
        for qq in range(4):
            kq, cq = qq % 2, 2 * k + qq // 2
            me = (k == kq) & (c == cq)
            for j, (s0, d0, n) in enumerate(((qq * 128, 0, 128), ((7 - qq) * 128, 128, 128), ((8 + 2 * qq) * 128, 256, 256))):
                s = src.at[pl.ds(s0, n), :]
                d = dst.at[c, pl.ds(d0, n), :]
                rs = R.irsem.at[which, c, j]
                cp = pltpu.make_async_remote_copy(
                    src_ref=s, dst_ref=d, send_sem=R.issem.at[which, qq, j], recv_sem=rs,
                    device_id=(a, 2 * y + kq, cq), device_id_type=MESH)
                sends.append((me, cp))

                @pl.when(jnp.logical_not(me))
                def _():
                    cp.start()

                @pl.when(me)
                def _():
                    pltpu.make_async_copy(s, d, rs).start()

        def wait():
            for cc in range(4):
                for j, (d0, n) in enumerate(((0, 128), (128, 128), (256, 256))):
                    d = dst.at[cc, pl.ds(d0, n), :]
                    pltpu.make_async_copy(d, d, R.irsem.at[which, cc, j]).wait()
        return sends, wait

    def rows_out(src, dst, which):
        sends = []
        for cc in range(4):
            me = (c // 2 == k) & (c == cc)
            for j, (s0, d0, n) in enumerate(((0, lo_row, 128), (128, hi_row, 128), (256, 1024 + pl.multiple_of(q * 256, 256), 256))):
                s = src.at[cc, pl.ds(s0, n), :]
                d = dst.at[pl.ds(d0, n), :]
                rs = R.irsem.at[which, q, j]
                cp = pltpu.make_async_remote_copy(
                    src_ref=s, dst_ref=d, send_sem=R.issem.at[which, cc, j], recv_sem=rs,
                    device_id=(a, owner_row, cc), device_id_type=MESH)
                sends.append((me, cp))

                @pl.when(jnp.logical_not(me))
                def _():
                    cp.start()

                @pl.when(me)
                def _():
                    pltpu.make_async_copy(s, d, rs).start()

        def wait():
            for qq in range(4):
                for j, (d0, n) in enumerate(((qq * 128, 128), ((7 - qq) * 128, 128), ((8 + 2 * qq) * 128, 256))):
                    d = dst.at[pl.ds(d0, n), :]
                    pltpu.make_async_copy(d, d, R.irsem.at[which, qq, j]).wait()
        return sends, wait

    def finish_sends(sends):
        for me, cp in sends:
            @pl.when(jnp.logical_not(me))
            def _():
                cp.wait_send()

    wst = {}

    def w_z(name):
        w = getattr(R, "w_" + name)
        here = w.at[y, k, c, :, ah]
        wst[name, "z"] = [send(here, here, (a, r, (c + i) % 4)) for i in range(1, 4)]

    def w_1(name):
        w = getattr(R, "w_" + name)
        for cp in wst[name, "z"]:
            cp.wait_recv()
        s = w.at[y, k, :, 0, ah]
        wst[name, "x1"] = send(s, s, xside)
        s = w.at[y, k, :, 1, ah]
        wst[name, "y1"] = send(s, s, yside)

    def w_2(name):
        w = getattr(R, "w_" + name)
        wst[name, "x1"].wait_recv()
        s = w.at[y, k, :, 0]
        wst[name, "y2"] = send(s, s, yside)
        wst[name, "y1"].wait_recv()
        s = w.at[:, k, :, 1, ah]
        wst[name, "x2"] = send(s, s, xside)

    def w_3(name):
        w = getattr(R, "w_" + name)
        wst[name, "y2"].wait_recv()
        wst[name, "x2"].wait_recv()
        s = w.at[:, k]
        wst[name, "core"] = send(s, s, core)

    def w_4(name):
        wst[name, "core"].wait_recv()

    gst = {}

    def add_into(dst, other, lead):
        for_index = [()]
        for n in lead:
            for_index = [ix + (i,) for ix in for_index for i in range(n)]
        for ix in for_index:
            dst[ix] = (dst[ix].astype(f32) + other(ix).astype(f32)).astype(bf16)

    def g_0(name):
        g, b0 = getattr(R, "g_" + name), getattr(R, "b0_" + name)
        gst[name, "core"] = send(g.at[:, 1 - k], b0, core)

    def g_1(name):
        g, b0, b1 = getattr(R, "g_" + name), getattr(R, "b0_" + name), getattr(R, "b1_" + name)
        gst[name, "core"].wait_recv()

        def one(i):
            yy, cc = i // 4, i % 4
            b0[yy, cc] = (b0[yy, cc].astype(f32) + g[yy, k, cc].astype(f32)).astype(bf16)
        loop(8, one)
        if use_x:
            b2 = getattr(R, "b2_" + name)
            gst[name, "y1"] = send(b0.at[1 - y, :, 0], b1, yside)
            gst[name, "x1"] = send(b0.at[:, :, 1, 1 - ah], b2, xside)
        else:
            gst[name, "y1"] = send(b0.at[1 - y], b1, yside)

    def g_2(name):
        b0, b1 = getattr(R, "b0_" + name), getattr(R, "b1_" + name)
        gst[name, "y1"].wait_recv()
        if not use_x:
            def one(cc):
                b1[cc] = (b1[cc].astype(f32) + b0[y, cc].astype(f32)).astype(bf16)
            loop(4, one)
            return
        b2, b3, b4 = (getattr(R, "b%d_%s" % (i, name)) for i in (2, 3, 4))

        def one(cc):
            b1[cc] = (b1[cc].astype(f32) + b0[y, cc, 0].astype(f32)).astype(bf16)
        loop(4, one)
        gst[name, "x2"] = send(b1.at[:, 1 - ah], b3, xside)
        gst[name, "x1"].wait_recv()

        def two(i):
            yy, cc = i // 4, i % 4
            b2[yy, cc] = (b2[yy, cc].astype(f32) + b0[yy, cc, 1, ah].astype(f32)).astype(bf16)
        loop(8, two)
        gst[name, "y2"] = send(b2.at[1 - y], b4, yside)

    def g_3(name):
        b1, z, b5 = (getattr(R, "%s_%s" % (i, name)) for i in ("b1", "z" if use_x else "b1", "b5"))
        if use_x:
            b2, b3, b4 = (getattr(R, "b%d_%s" % (i, name)) for i in (2, 3, 4))
            gst[name, "x2"].wait_recv()
            gst[name, "y2"].wait_recv()

            def one(cc):
                z[cc, 0] = (b1[cc, ah].astype(f32) + b3[cc].astype(f32)).astype(bf16)
                z[cc, 1] = (b2[y, cc].astype(f32) + b4[cc].astype(f32)).astype(bf16)
            loop(4, one)
        gst[name, "z"] = [send(z.at[(c + i) % 4], b5.at[i - 1], (a, r, (c + i) % 4)) for i in range(1, 4)]

    def g_4(name):
        z, b5, fin = (getattr(R, "%s_%s" % (i, name)) for i in ("z" if use_x else "b1", "b5", "fin"))
        for cp in gst[name, "z"]:
            cp.wait_recv()
        if use_x:
            for t in range(2):
                total = z[c, t].astype(f32)
                for i in range(3):
                    total = total + b5[i, t].astype(f32)
                fin[t, ah] = total.astype(bf16)
            s = fin.at[:, ah]
            gst[name, "x3"] = send(s, s, xside)
        else:
            for t in range(2):
                for i2 in range(2):
                    total = z[c, t, i2].astype(f32)
                    for i in range(3):
                        total = total + b5[i, t, i2].astype(f32)
                    fin[t, i2] = total.astype(bf16)

    def g_5(name):
        fin = getattr(R, "fin_" + name)
        if use_x:
            gst[name, "x3"].wait_recv()
        rows, cols = BLOCK[name]
        return fin[...].reshape(rows, cols).astype(f32)

    def weight(name, rr):
        w = getattr(R, "w_" + name)
        return w[rr // 2, rr % 2].reshape(4 * BLOCK[name][0], BLOCK[name][1])

    R.vecs[c] = R.vec[...]
    R.vecr[r] = R.vec[...]
    vec_cp = [send(R.vec, R.vecs.at[c], (a, r, (c + i) % 4)) for i in range(1, 4)]
    vec_cp += [send(R.vec, R.vecr.at[r], dev) for dev in (core, yside, diag)]
    w_z("qkv")
    tok_sends, tok_wait = rows_in(R.tok, R.xo, 0)
    for cp in local[1:]:
        cp.wait()
    w_z("og")
    w_1("qkv")
    w_z("up")
    w_2("qkv")
    w_z("dg")
    for cp in vec_cp:
        cp.wait_recv()

    def vec_row(i):
        return cat([R.vecs[cc, i:i + 1, :] for cc in range(4)])

    tok_wait()

    def xrows():
        return cat([R.xo[cc] for cc in range(4)]).astype(f32)

    def norm_parts(v):
        mean = jnp.sum(v, axis=1, keepdims=True) * (1.0 / D)
        cen = v - mean
        var = jnp.sum(cen * cen, axis=1, keepdims=True) * (1.0 / D)
        inv = lax.rsqrt(var + EPS)
        return cen * inv, inv

    standard, _ = norm_parts(xrows())
    n1 = (standard * vec_row(0) + vec_row(1)).astype(bf16)
    R.n1[...] = n1
    R.xn[pl.ds(lo_row, 128), :] = n1[0:128]
    R.xn[pl.ds(hi_row, 128), :] = n1[128:256]
    R.xn[1024:1280, :] = n1[256:512]
    here = [R.xn.at[pl.ds(lo_row, 128), :], R.xn.at[pl.ds(hi_row, 128), :]]
    to_z = [send(s, s, zside) for s in here]
    to_core = [send(s, s, core) for s in here]
    w_3("qkv")
    w_1("og")
    w_2("og")
    cot_sends, cot_wait = rows_in(R.cot, R.co, 1)
    qz = q + 2 - 4 * (q // 2)
    for cp in to_z:
        cp.wait_recv()
    there = [R.xn.at[pl.ds(pl.multiple_of(qz * 128, 128), 128), :],
             R.xn.at[pl.ds(pl.multiple_of((7 - qz) * 128, 128), 128), :]]
    to_core += [send(s, s, core) for s in there]
    w_4("qkv")
    for cp in to_core:
        cp.wait_recv()

    def qkv_pair(p):
        w = weight("qkv", p)
        R.qp[p] = (dot(R.n1[...], w[:, 0:128], 1, 0).astype(bf16).astype(f32) * 0.125).astype(bf16)
        R.kv[p] = dot(R.xn[...], w[:, 128:384], 1, 0).astype(bf16)
    loop(4, qkv_pair)
    w_3("og")
    w_1("up")
    w_1("dg")

    lane = lax.broadcasted_iota(jnp.int32, (T, 128), 1)
    key_at = lax.broadcasted_iota(jnp.int32, (512, 128), 0)
    col_at = lax.broadcasted_iota(jnp.int32, (512, 128), 1)
    lo_ok = key_at <= col_at + q * 128
    hi_ok = key_at + 512 <= col_at + (7 - q) * 128
    own_ok = (key_at <= col_at)[0:128]

    def attend_pair(p):
        for h in range(2):
            keys = R.kv[p, :, 0:128]
            vals = R.kv[p, :, 128:256]
            qm = jnp.where(lane // 64 == h, R.qp[p], jnp.zeros((), bf16))
            s1 = dot(keys[0:512], qm, 1, 1)
            s2 = dot(keys[512:1024], qm[128:512], 1, 1)
            sa = jnp.where(own_ok, dot(keys[1024:1152], qm[256:384], 1, 1), MASKED)
            sb = jnp.where(own_ok, dot(keys[1152:1280], qm[384:512], 1, 1), MASKED)
            s1 = cat([jnp.where(lo_ok, s1[:, 0:128], MASKED), s1[:, 128:512]])
            s2 = cat([jnp.where(hi_ok, s2[:, 0:128], MASKED), s2[:, 128:384]])
            top = lambda v: jnp.max(v, axis=0, keepdims=True)
            add = lambda v: jnp.sum(v, axis=0, keepdims=True)
            m1 = top(s1)
            m2 = jnp.maximum(m1[:, 128:512], top(s2))
            m = cat([m1[:, 0:128], m2[:, 0:128], jnp.maximum(m2[:, 128:384], cat([top(sa), top(sb)]))])
            e1 = jnp.exp(s1 - m)
            e2 = jnp.exp(s2 - m[:, 128:512])
            ea = jnp.exp(sa - m[:, 256:384])
            eb = jnp.exp(sb - m[:, 384:512])
            l1 = add(e1)
            l2 = l1[:, 128:512] + add(e2)
            total = cat([l1[:, 0:128], l2[:, 0:128], l2[:, 128:384] + cat([add(ea), add(eb)])])
            e1, e2, ea, eb = (v.astype(bf16) for v in (e1, e2, ea, eb))
            R.p1[2 * p + h] = e1
            R.p2[2 * p + h] = e2
            R.po[2 * p + h, :, 0:128] = ea
            R.po[2 * p + h, :, 128:256] = eb
            o1 = dot(vals[0:512], e1, 0, 0)
            o2 = dot(vals[512:1024], e2, 0, 0)
            oa = dot(vals[1024:1152], ea, 0, 0)
            ob = dot(vals[1152:1280], eb, 0, 0)
            o2 = o1[:, 128:512] + o2
            o = cat([o1[:, 0:128], o2[:, 0:128], o2[:, 128:384] + cat([oa, ob])])
            inv = 1.0 / total
            R.li[p, h:h + 1, :] = inv
            R.att[p, 64 * h:64 * h + 64, :] = (o[64 * h:64 * h + 64] * inv).astype(bf16)
    loop(4, attend_pair)
    w_4("og")
    w_2("up")
    w_2("dg")

    def lanes(cc):
        return pl.ds(pl.multiple_of(cc * 128, 128), 128)

    def wide(cc):
        return pl.ds(pl.multiple_of(cc * 256, 256), 256)

    def out_block(cc):
        w = R.w_og[:, :, cc].reshape(512, 256)
        br = dot(R.att[...].reshape(512, T), w, 0, 0)
        ao = br[:, 0:128]
        gate = sigmoid(br[:, 128:256] + R.vecs[cc, 2:3, :])
        R.ao[cc] = ao
        R.g1[cc] = gate
        R.mid[cc] = R.xo[cc].astype(f32) + gate * ao
    loop(4, out_block)

    def midrows():
        return cat([R.mid[cc] for cc in range(4)])

    standard, _ = norm_parts(midrows())
    R.n2[...] = (standard * vec_row(3) + vec_row(4)).astype(bf16)
    w_3("up")
    w_3("dg")
    w_4("up")

    def up_block(rr):
        pre = dot(R.n2[...], weight("up", rr), 1, 0) + cat([R.vecr[rr, 8 + i:9 + i, :] for i in range(4)])
        s = sigmoid(pre)
        R.hid[rr] = (pre * s).astype(bf16)
        R.slp[rr] = (s * (1.0 + pre * (1.0 - s))).astype(bf16)
    loop(4, up_block)
    w_4("dg")
    cot_wait()

    def down_block(cc):
        br = dot(R.hid[0], R.w_dg[0, 0, cc].reshape(512, 256), 1, 0)
        for rr in range(1, 4):
            br = br + dot(R.hid[rr], R.w_dg[rr // 2, rr % 2, cc].reshape(512, 256), 1, 0)
        ffn = br[:, 0:128] + R.vecs[cc, 5:6, :]
        gate = sigmoid(br[:, 128:256] + R.vecs[cc, 6:7, :])
        R.out[cc] = (R.mid[cc] + gate * ffn).astype(bf16)
        g = R.co[cc].astype(f32)
        gf = (g * gate).astype(bf16)
        gg = (g * ffn * gate * (1.0 - gate)).astype(bf16)
        R.pair[cc, :, 0:128] = gf
        R.pair[cc, :, 128:256] = gg
        R.sv[5, pl.ds(cc, 1), :] = jnp.sum(gf.astype(f32), axis=0, keepdims=True)
        R.sv[6, pl.ds(cc, 1), :] = jnp.sum(gg.astype(f32), axis=0, keepdims=True)
    loop(4, down_block)
    out_sends, out_wait = rows_out(R.out, R.out_o, 2)

    def grad_down(i):
        rr, cc = i // 4, i % 4
        R.g_dg[rr // 2, rr % 2, cc] = dot(R.hid[rr], R.pair[cc], 0, 0).astype(bf16).reshape(2, 2, 128, 256)
    loop(16, grad_down)
    g_0("dg")

    def back_up(rr):
        gh = dot(R.pair[0], R.w_dg[rr // 2, rr % 2, 0].reshape(512, 256), 1, 1)
        for cc in range(1, 4):
            gh = gh + dot(R.pair[cc], R.w_dg[rr // 2, rr % 2, cc].reshape(512, 256), 1, 1)
        gp = (gh * R.slp[rr].astype(f32)).astype(bf16)
        R.slp[rr] = gp
        tot = jnp.sum(gp.astype(f32), axis=0, keepdims=True)
        for i in range(4):
            R.sv[8 + rr, i:i + 1, :] = tot[:, 128 * i:128 * i + 128]
    loop(4, back_up)
    g_1("dg")

    def grad_up(rr):
        R.g_up[rr // 2, rr % 2] = dot(R.n2[...], R.slp[rr], 0, 0).astype(bf16).reshape(4, 2, 2, 32, 512)
    loop(4, grad_up)
    g_0("up")

    gn = dot(R.slp[0], weight("up", 0), 1, 1)
    for rr in range(1, 4):
        gn = gn + dot(R.slp[rr], weight("up", rr), 1, 1)

    def norm_back(v, grad, gain_row, at):
        std, inv = norm_parts(v)
        gs = jnp.sum(grad * std, axis=0, keepdims=True)
        gb = jnp.sum(grad, axis=0, keepdims=True)
        for cc in range(4):
            R.sv[at, cc:cc + 1, :] = gs[:, 128 * cc:128 * cc + 128]
            R.sv[at + 1, cc:cc + 1, :] = gb[:, 128 * cc:128 * cc + 128]
        s = grad * vec_row(gain_row)
        f = jnp.sum(s, axis=1, keepdims=True) * (1.0 / D)
        e = jnp.sum(s * std, axis=1, keepdims=True) * (1.0 / D)
        return inv * (s - f - std * e)

    gm = norm_back(midrows(), gn, 3, 2)
    for cc in range(4):
        g_mid = R.co[cc].astype(f32) + gm[:, 128 * cc:128 * cc + 128]
        R.gm[cc] = g_mid
        gate = R.g1[cc]
        ga = (g_mid * gate).astype(bf16)
        gg = (g_mid * R.ao[cc] * gate * (1.0 - gate)).astype(bf16)
        R.pair[cc, :, 0:128] = ga
        R.pair[cc, :, 128:256] = gg
        R.sv[4, cc:cc + 1, :] = jnp.sum(gg.astype(f32), axis=0, keepdims=True)
    g_1("up")

    def grad_out(cc):
        R.g_og[:, :, cc] = dot(R.att[...].reshape(512, T), R.pair[cc], 1, 0).astype(bf16).reshape(2, 2, 2, 2, 32, 256)
    loop(4, grad_out)
    g_0("og")
    g_2("dg")
    do = dot(R.w_og[:, :, 0].reshape(512, 256), R.pair[0], 1, 1)
    for cc in range(1, 4):
        do = do + dot(R.w_og[:, :, cc].reshape(512, 256), R.pair[cc], 1, 1)
    for cc in range(4):
        R.mid[cc] = do[:, 128 * cc:128 * cc + 128]
    g_1("og")
    g_2("up")
    g_3("dg")

    row_of = lax.broadcasted_iota(jnp.int32, (128, T), 0)

    def back_pair(p):
        rows = pl.ds(pl.multiple_of(p * 128, 128), 128)
        dot_t = cat([R.mid[cc, rows, :] for cc in range(4)])
        dot_t = dot_t * jnp.where(row_of < 64, R.li[p, 0:1, :], R.li[p, 1:2, :])
        prod = dot_t * R.att[p].astype(f32)
        dot_t = dot_t.astype(bf16)
        dot_n = dot_t.T
        keys = R.kv[p, :, 0:128]
        vals = R.kv[p, :, 128:256]
        grads = []
        queries = []
        for h in range(2):
            delta = jnp.sum(prod[64 * h:64 * h + 64], axis=0, keepdims=True)
            qm = jnp.where(lane // 64 == h, R.qp[p], jnp.zeros((), bf16))
            om = jnp.where(lane // 64 == h, dot_n, jnp.zeros((), bf16))
            omt = jnp.where(row_of // 64 == h, dot_t, jnp.zeros((), bf16))
            e1, e2 = R.p1[2 * p + h], R.p2[2 * p + h]
            ea, eb = R.po[2 * p + h, :, 0:128], R.po[2 * p + h, :, 128:256]
            d1 = (e1.astype(f32) * (dot(vals[0:512], omt, 1, 0) - delta)).astype(bf16)
            d2 = (e2.astype(f32) * (dot(vals[512:1024], omt[:, 128:512], 1, 0) - delta[:, 128:512])).astype(bf16)
            da = (ea.astype(f32) * (dot(vals[1024:1152], omt[:, 256:384], 1, 0) - delta[:, 256:384])).astype(bf16)
            db = (eb.astype(f32) * (dot(vals[1152:1280], omt[:, 384:512], 1, 0) - delta[:, 384:512])).astype(bf16)
            dk = cat([dot(d1, qm, 1, 0), dot(d2, qm[128:512], 1, 0), dot(da, qm[256:384], 1, 0), dot(db, qm[384:512], 1, 0)], 0)
            dv = cat([dot(e1, om, 1, 0), dot(e2, om[128:512], 1, 0), dot(ea, om[256:384], 1, 0), dot(eb, om[384:512], 1, 0)], 0)
            grads.append((dk, dv))
            x1 = dot(keys[0:512], d1, 0, 0)
            x2 = x1[:, 128:512] + dot(keys[512:1024], d2, 0, 0)
            xab = cat([dot(keys[1024:1152], da, 0, 0), dot(keys[1152:1280], db, 0, 0)])
            dq = cat([x1[:, 0:128], x2[:, 0:128], x2[:, 128:384] + xab])
            queries.append(dq[64 * h:64 * h + 64])
        R.kv[p, :, 0:128] = (grads[0][0] + grads[1][0]).astype(bf16)
        R.kv[p, :, 128:256] = (grads[0][1] + grads[1][1]).astype(bf16)
        R.qp[p] = (cat(queries, 0) * 0.125).astype(bf16).T
    loop(4, back_pair)
    g_2("og")
    g_3("up")
    g_4("dg")

    def back_rows(first, count):
        rows = pl.ds(first, count)
        total = dot(R.kv[0, rows, :], weight("qkv", 0)[:, 128:384], 1, 1)
        for p in range(1, 4):
            total = total + dot(R.kv[p, rows, :], weight("qkv", p)[:, 128:384], 1, 1)
        return total

    def chunk_rows(qq):
        return (pl.multiple_of(qq * 128, 128), pl.multiple_of((7 - qq) * 128, 128))

    q1 = q + 1 - 2 * k
    q2 = qz
    q3 = q2 + 1 - 2 * k
    for i, row in enumerate(chunk_rows(q1)):
        R.ex[0, 128 * i:128 * i + 128, :] = back_rows(row, 128).astype(bf16)
    for i, row in enumerate(chunk_rows(q3)):
        R.ex[1, 128 * i:128 * i + 128, :] = back_rows(row, 128).astype(bf16)
    part_core = send(R.ex, R.exr, core)
    mine2 = [back_rows(row, 128) for row in chunk_rows(q2)]
    part_core.wait_recv()
    for i in range(2):
        R.ez[128 * i:128 * i + 128, :] = (mine2[i] + R.exr[1, 128 * i:128 * i + 128, :].astype(f32)).astype(bf16)
    part_z = send(R.ez, R.ezr, zside)

    def grad_qkv(p):
        g = cat([dot(R.n1[...], R.qp[p], 0, 0), dot(R.xn[...], R.kv[p], 0, 0)]).astype(bf16)
        R.g_qkv[p // 2, p % 2] = g.reshape(4, 2, 2, 32, 384)
    loop(4, grad_qkv)
    g_0("qkv")
    g_3("og")
    g_4("up")

    for row, n, at in ((lo_row, 128, 0), (hi_row, 128, 128), (1024, 256, 256)):
        own = back_rows(row, n)
        for cc in range(4):
            R.mid[cc, at:at + n, :] = own[:, 128 * cc:128 * cc + 128]

    def add_queries(p):
        more = dot(R.qp[p], weight("qkv", p)[:, 0:128], 1, 1)
        for cc in range(4):
            R.mid[cc] = R.mid[cc] + more[:, 128 * cc:128 * cc + 128]
    loop(4, add_queries)
    g_1("qkv")
    part_z.wait_recv()
    for cc in range(4):
        here = slice(128 * cc, 128 * cc + 128)
        R.mid[cc, 0:256, :] = R.mid[cc, 0:256, :] + (R.exr[0, :, here].astype(f32) + R.ezr[:, here].astype(f32))
    gx = norm_back(xrows(), midrows(), 0, 0)
    for cc in range(4):
        R.ing[cc] = (R.gm[cc] + gx[:, 128 * cc:128 * cc + 128]).astype(bf16)
    ing_sends, ing_wait = rows_out(R.ing, R.ing_o, 3)
    g_2("qkv")
    g_3("qkv")

    s1 = send(R.sv, R.svr.at[0], core)
    s1.wait_recv()
    R.sv2[...] = R.sv[...] + R.svr[0]
    s2 = send(R.sv2, R.svr.at[1], yside)
    g_4("og")
    s2.wait_recv()
    R.sv3[...] = R.sv2[...] + R.svr[1]
    if use_x:
        s3 = send(R.sv3, R.svr.at[2], xside)
        g_4("qkv")
        s3.wait_recv()
        R.sv4[...] = R.sv3[...] + R.svr[2]
    else:
        g_4("qkv")
        R.sv4[...] = R.sv3[...]
    s4 = [send(R.sv4, R.svr.at[2 + i], (a, r, (c + i) % 4)) for i in range(1, 4)]

    R.dg_o[...] = g_5("dg")
    R.up_o[...] = g_5("up")
    R.og_o[...] = g_5("og")
    g = g_5("qkv")
    R.qkv_o[...] = cat([g[:, (2 * j + h) * 64:(2 * j + h + 1) * 64] for h in range(2) for j in range(3)])
    for cp in s4:
        cp.wait_recv()
    R.svr[2] = R.sv4[...]
    R.small_o[...] = jnp.zeros((16, 128), f32)
    order = [2 + lax.rem(c - cc + 4, 4) for cc in range(4)]

    def total_of(i, j):
        v = R.svr[order[0], i, pl.ds(j, 1), :]
        for cc in range(1, 4):
            v = v + R.svr[order[cc], i, pl.ds(j, 1), :]
        return v
    for i in range(7):
        R.small_o[i:i + 1, :] = total_of(i, c)
    for i in range(4):
        R.small_o[8 + i:9 + i, :] = total_of(8 + r, i)

    out_wait()
    ing_wait()
    for cp in pending:
        cp.wait_send()
    for sends in (tok_sends, cot_sends, out_sends, ing_sends):
        finish_sends(sends)


def body(use_x, tokens, cotangent, norm1_gain, norm1_bias, qkv_weight, out_weight, gate1_weight,
         gate1_bias, norm2_gain, norm2_bias, up_weight, up_bias, down_weight, down_bias,
         gate2_weight, gate2_bias):
    vec = jnp.concatenate([norm1_gain, norm1_bias, gate1_bias, norm2_gain, norm2_bias, down_bias,
                           gate2_bias, jnp.zeros_like(gate2_bias), up_bias,
                           jnp.zeros((512,), bf16)]).astype(f32).reshape(16, 128)
    hbm = pl.BlockSpec(memory_space=pl.ANY)
    vmem = pl.BlockSpec(memory_space=pltpu.VMEM)
    ins = {"tok": tokens, "cot": cotangent, "i_qkv": qkv_weight, "i_out": out_weight, "i_gate1": gate1_weight,
           "i_up": up_weight, "i_down": down_weight, "i_gate2": gate2_weight, "vec": vec}
    outs = {"out_o": ((2048, 128), bf16, hbm), "ing_o": ((2048, 128), bf16, hbm),
            "qkv_o": ((128, 384), f32, vmem), "og_o": ((128, 256), f32, vmem),
            "up_o": ((128, 512), f32, vmem), "dg_o": ((512, 256), f32, vmem),
            "small_o": ((16, 128), f32, vmem)}
    scr = {}
    for name in NAMES:
        rows, cols = BLOCK[name]
        rq = rows // 4
        scr["w_" + name] = ((2, 2, 4, 2, 2, rq, cols), bf16)
        scr["g_" + name] = ((2, 2, 4, 2, 2, rq, cols), bf16)
        scr["b0_" + name] = ((2, 4, 2, 2, rq, cols), bf16)
        if use_x:
            scr["b1_" + name] = ((4, 2, rq, cols), bf16)
            scr["b2_" + name] = ((2, 4, rq, cols), bf16)
            scr["b3_" + name] = ((4, rq, cols), bf16)
            scr["b4_" + name] = ((4, rq, cols), bf16)
            scr["z_" + name] = ((4, 2, rq, cols), bf16)
            scr["b5_" + name] = ((3, 2, rq, cols), bf16)
        else:
            scr["b1_" + name] = ((4, 2, 2, rq, cols), bf16)
            scr["b5_" + name] = ((3, 2, 2, rq, cols), bf16)
        scr["fin_" + name] = ((2, 2, rq, cols), bf16)
    scr.update({
        "qstage": ((128, 384), bf16), "vecs": ((4, 16, 128), f32), "vecr": ((4, 16, 128), f32),
        "xo": ((4, T, 128), bf16), "co": ((4, T, 128), bf16), "n1": ((T, D), bf16),
        "xn": ((1280, D), bf16), "qp": ((4, T, 128), bf16), "kv": ((4, 1280, 256), bf16),
        "p1": ((8, 512, 512), bf16), "p2": ((8, 512, 384), bf16), "po": ((8, 128, 256), bf16),
        "li": ((4, 8, T), f32), "att": ((4, 128, T), bf16), "ao": ((4, T, 128), f32),
        "g1": ((4, T, 128), f32), "mid": ((4, T, 128), f32), "n2": ((T, D), bf16),
        "hid": ((4, T, 512), bf16), "slp": ((4, T, 512), bf16), "out": ((4, T, 128), bf16),
        "pair": ((4, T, 256), bf16), "gm": ((4, T, 128), f32), "ing": ((4, T, 128), bf16),
        "ex": ((2, 256, D), bf16), "exr": ((2, 256, D), bf16), "ez": ((256, D), bf16), "ezr": ((256, D), bf16),
        "sv": ((12, 8, 128), f32), "sv2": ((12, 8, 128), f32), "sv3": ((12, 8, 128), f32),
        "sv4": ((12, 8, 128), f32), "svr": ((6, 12, 8, 128), f32),
    })
    shapes = [pltpu.VMEM(s, d) for s, d in scr.values()]
    names_scr = tuple(scr) + ("ssem", "rsem", "issem", "irsem", "lsem")
    n_sem = 104
    dma = pltpu.SemaphoreType.DMA
    shapes += [dma((n_sem,)), dma((n_sem,)), dma((4, 4, 3)), dma((4, 4, 3)), dma((16,))]
    res = pl.pallas_call(
        partial(kernel, use_x, tuple(ins), tuple(outs), names_scr),
        out_shape=[jax.ShapeDtypeStruct(s, d) for s, d, _ in outs.values()],
        in_specs=[hbm] * 8 + [vmem],
        out_specs=[sp for _, _, sp in outs.values()],
        scratch_shapes=shapes,
        compiler_params=pltpu.CompilerParams(collective_id=0, has_side_effects=True, vmem_limit_bytes=60 * 1024 * 1024),
    )(*ins.values())
    output, input_grad, gq, gog, gup, gdg, small = res
    if not use_x:
        gq, gog, gup, gdg, small = lax.psum((gq, gog, gup, gdg, small), "grp")
    return (output, input_grad, small[0], small[1], gq, gog[:, :128], gog[:, 128:], small[4], small[2],
            small[3], gup, small[8:12].reshape(512), gdg[:, :128], small[5], gdg[:, 128:], small[6])


def solution(mesh):
    act = P(("grp", "row"), "col")
    col, row = P("col"), P("row")
    cr, rc = P("col", "row"), P("row", "col")
    return jax.shard_map(
        partial(body, mesh.shape["grp"] == 2),
        mesh=mesh,
        in_specs=(act, act, col, col, cr, rc, rc, col, col, col, cr, row, rc, col, rc, col),
        out_specs=(act, act, col, col, cr, rc, rc, col, col, col, cr, row, rc, col, rc, col),
        check_vma=False,
    )
```

time: 1970 us -> 190 us (0.10)
  waiting for transfers between devices: 1640 us -> 0 us
  Pallas kernels: 0 us -> 173 us
  blocking collectives: 116 us -> 0 us
  matrix products: 109 us -> 0 us
  other arithmetic: 64.7 us -> 0.6 us
    reduce_scatter x8 -> x0, waiting for transfers between devices: 1070 us -> none  [the longest x4 846 us: sum_cols(): lax.psum_scatter(term(jnp.int32(0), rows_here * lax.axis_size('col')), 'c...]
    all_gather x8 -> x0, waiting for transfers between devices: 552 us -> none  [the longest x4 445 us: cols_whole(): return lax.all_gather(values, 'col', axis=0, tiled=True)]
    pallas_call x0 -> x1, Pallas kernels: none -> 173 us  [body(): pl.pallas_call(partial(kernel, use_x, tuple(ins), tuple(outs), names_scr)...]
    psum x5 -> x0, blocking collectives: 116 us -> none  [the longest x4 76.6 us: col_totals(): return lax.psum((first_sum, second_sum), 'col')]
    dot_general x36 -> x0, matrix products: 109 us -> none  [the longest x4 32.7 us: times_plain(): return jnp.dot(left_side, right, preferred_element_type=jnp.float32)]
    convert_element_type x21 -> x1, other arithmetic: 31.6 us -> 0.6 us  [body(): vec = jnp.concatenate([norm1_gain, norm1_bias, gate1_bias, norm2_gain, no...]
    reduce_sum x11 -> x0, other arithmetic: 26.9 us -> none  [the longest x1 5.91 us: body(): up_bias_sum = place_rows(jnp.sum(grad_up_rows, axis=0, dtype=jnp.float32))]
  transfers between devices with their start and end apart: 17 -> 0, of which waited for: 17 -> 0; matrix products, arithmetic and copies ran while one was open for 2% -> 0% of each run, Pallas kernels for 0% -> 0%
where the time goes in v1:
time: 190 us
  Pallas kernels  173 us (91%)
  local copies, waits for them, and re-layouts  15.1 us (8%)
    pallas_call x1, Pallas kernels, body(): pl.pallas_call(partial(kernel, use_x, tuple(ins), tuple(outs), names_scr)...  173 us
    unnamed x39, local copies, waits for them, and re-layouts  10.4 us

profile of v1, /device:TPU:0, one launch (start us, length us, event | category | flops | bytes accessed | tf_op | source)
XLA Modules:
  0.0 189.9 jit_solution(282707885579408502)
XLA Ops:
  0.7 0.6 copy-done.6
  1.5 0.5 copy-done.7
  2.1 0.5 copy-done.8
  2.8 0.5 copy-done.9
  3.5 0.5 copy-done.10
  4.1 0.5 copy-done.11
  4.8 0.5 copy-done.12
  5.4 0.2 dynamic-update-slice.7
  5.7 0.4 copy-done.5
  6.3 0.2 dynamic-update-slice.9
  6.5 0.6 bitcast_convert_fusion.refs_8_
  7.1 173.4 %shard_map.279 = (bf16[2048,128]{1,0:T(8,128)(2,1)}, bf16[2048,128]{1,0:T(8,128)(2,1)}, f32[128,384]{1,0:T(8,128)}, f32[128,256]{1,0:T(8,128)}, f32[128,512]{1,0...) custom-call(bf16[2048,128]{1,0:T(8,128)(2,1)} %refs_0_.1, bf16[2048,128]{1,0:T(8,128)(2,1)} %refs_1_.1, ...), custom_call_target="tpu_custom_call" | custom-call | tf_op jit(solution)/shard_map/pallas_call | solution.py:717
  180.5 0.7 copy-done.4
  181.2 0.6 slice_bitcast_fusion
  181.8 0.5 slice_bitcast_fusion.1
  182.3 1.5 fusion.1
  183.9 1.9 %fusion = (f32[512,128]{1,0:T(8,128)}, f32[512,128]{1,0:T(8,128)}) fusion(f32[512,256]{1,0:T(8,128)} %get-tuple-element.29), kind=kLoop, calls=%fused_computation.9 | loop fusion | bytes 1048576 | tf_op jit(solution)/shard_map/slice | solution.py:729
  185.8 0.8 copy.46
  186.6 0.4 copy-done
  187.0 0.8 copy.47
  187.8 0.3 copy-done.3
  188.1 0.7 copy.48
  188.8 0.3 copy-done.2
  189.2 0.7 copy.49
  (25 shorter events, 1.5 us)
Async XLA Ops:
  0.6 0.7 copy-start.6
  1.3 0.7 copy-start.7
  2.0 0.7 copy-start.8
  2.6 0.7 copy-start.9
  3.3 0.7 copy-start.10
  3.9 0.7 copy-start.11
  4.6 0.7 copy-start.12
  5.4 0.7 copy-start.5
  180.5 0.7 copy-start.4
  183.9 1.9 %copy-start.1 = (bf16[2048,128]{1,0:T(8,128)(2,1)S(1)}, bf16[2048,128]{1,0:T(8,128)(2,1)}, u32[]{:S(2)}) copy-start(bf16[2048,128]{1,0:T(8,128)(2,1)} %get-tuple-element.57) | copy-start | bytes 1572868
  185.8 1.2 copy-start
  187.0 1.1 copy-start.3
  188.1 1.0 copy-start.2

commit v2 on v1

--- a/solution.py
+++ b/solution.py
@@ -15,8 +15,9 @@
 
 T = 512
 D = 512
-BLOCK = {"qkv": (128, 384), "og": (128, 256), "up": (128, 512), "dg": (512, 256)}
-NAMES = ("qkv", "og", "up", "dg")
+BLOCK = {"qkv": (128, 384), "og": (128, 256), "up": (128, 512), "d0": (256, 256), "d1": (256, 256)}
+NAMES = ("qkv", "og", "up", "d0", "d1")
+VECTORS = ("norm1_gain", "norm1_bias", "gate1_bias", "norm2_gain", "norm2_bias", "down_bias", "gate2_bias")
 
 
 def dot(a, b, ca, cb):
@@ -29,6 +30,17 @@
 
 def cat(parts, axis=1):
     return jnp.concatenate(parts, axis=axis)
+
+
+class Waiter:
+    def __init__(self, make):
+        self.make = make
+
+    def wait_recv(self):
+        self.make().wait_recv()
+
+    def wait_send(self):
+        self.make().wait_send()
 
 
 def sigmoid(v):
@@ -44,6 +56,8 @@
     y, k = r // 2, r % 2
     ah = a % 2
     q = 2 * (c % 2) + k
+    y_, k_, a_ = 1 - y, 1 - k, 1 - ah
+    others = [lax.rem(c + i, 4) for i in range(1, 4)]
     core = (a, 2 * y + 1 - k, c)
     yside = (a, 2 * (1 - y) + k, c)
     xside = (a + 1 - 2 * ah, r, c)
@@ -58,12 +72,14 @@
     def send(src, dst, dev):
         i = counter[0]
         counter[0] += 1
-        cp = pltpu.make_async_remote_copy(
-            src_ref=src, dst_ref=dst, send_sem=R.ssem.at[i], recv_sem=R.rsem.at[i],
-            device_id=dev, device_id_type=MESH)
-        cp.start()
-        pending.append(cp)
-        return cp
+
+        def make():
+            return pltpu.make_async_remote_copy(
+                src_ref=src() if callable(src) else src, dst_ref=dst() if callable(dst) else dst,
+                send_sem=R.ssem.at[i], recv_sem=R.rsem.at[i], device_id=dev, device_id_type=MESH)
+        make().start()
+        pending.append(Waiter(make))
+        return pending[-1]
 
     local = []
 
@@ -74,18 +90,18 @@
 
     fetch(R.i_qkv, R.qstage)
     for t in range(2):
-        for name, sources in (("og", ("out", "gate1")), ("up", ("up",)), ("dg", ("down", "gate2"))):
+        for name, sources, skip in (("og", ("out", "gate1"), 0), ("up", ("up",), 0),
+                                    ("d0", ("down", "gate2"), 0), ("d1", ("down", "gate2"), 256)):
             rows, cols = BLOCK[name]
             rq = rows // 4
             w = getattr(R, "w_" + name)
             width = cols // len(sources)
             for j, s in enumerate(sources):
-                at = pl.multiple_of((2 * t + ah) * rq, 32)
+                at = pl.multiple_of((2 * t + ah) * rq + skip, 32)
                 fetch(getattr(R, "i_" + s).at[pl.ds(at, rq), :],
                       w.at[y, k, c, t, ah, :, pl.ds(j * width, width)])
 
     barrier = pltpu.get_barrier_semaphore()
-    friends = [(a, 2 * y + kk, cc) for kk in range(2) for cc in range(4)]
     for kk in range(2):
         for cc in range(4):
             me = (k == kk) & (c == cc)
@@ -94,7 +110,9 @@
             def _():
                 pl.semaphore_signal(barrier, inc=1, device_id=(a, 2 * y + kk, cc), device_id_type=MESH)
     diag = (a, 2 * (1 - y) + 1 - k, c)
-    for dev in (yside, xside, diag):
+    corners = [(g, rr, c) for g in ((a, a + 1 - 2 * ah) if use_x else (a,))
+               for rr in (r, 2 * y + 1 - k, 2 * (1 - y) + k, 2 * (1 - y) + 1 - k)][1:]
+    for dev in (corners[1:] if use_x else corners[1:] + [xside]):
         pl.semaphore_signal(barrier, inc=1, device_id=dev, device_id_type=MESH)
 
     local[0].wait()
@@ -102,7 +120,12 @@
         blk = R.qstage[pl.ds(pl.multiple_of((2 * t + ah) * 32, 32), 32), :].astype(f32)
         parts = [blk[:, (3 * h + j) * 64:(3 * h + j + 1) * 64] for j in range(3) for h in range(2)]
         R.w_qkv[y, k, c, t, ah] = cat(parts).astype(bf16)
-    pl.semaphore_wait(barrier, 10)
+    R.vec[...] = jnp.zeros((16, 128), f32)
+    for i, name in enumerate(VECTORS):
+        R.vec[i:i + 1, :] = getattr(R, name)[...].astype(f32).reshape(1, 128)
+    for i in range(4):
+        R.vec[8 + i:9 + i, :] = R.up_bias[128 * i:128 * i + 128].astype(f32).reshape(1, 128)
+    pl.semaphore_wait(barrier, 13 if use_x else 10)
 
     def rows_in(src, dst, which):
         sends = []
@@ -171,53 +194,54 @@
 
     def w_z(name):
         w = getattr(R, "w_" + name)
-        here = w.at[y, k, c, :, ah]
-        wst[name, "z"] = [send(here, here, (a, r, (c + i) % 4)) for i in range(1, 4)]
+        here = lambda: w.at[y, k, c, :, ah]
+        wst[name, "z"] = [send(here, here, (a, r, cc)) for cc in others]
+
+    def to_sibling(name, s):
+        wst.setdefault((name, "core"), []).append(send(s, s, core))
 
     def w_1(name):
         w = getattr(R, "w_" + name)
         for cp in wst[name, "z"]:
             cp.wait_recv()
-        s = w.at[y, k, :, 0, ah]
+        s = lambda: w.at[y, k, :, 0, ah]
         wst[name, "x1"] = send(s, s, xside)
-        s = w.at[y, k, :, 1, ah]
+        s = lambda: w.at[y, k, :, 1, ah]
         wst[name, "y1"] = send(s, s, yside)
+        to_sibling(name, lambda: w.at[y, k, :, :, ah])
 
     def w_2(name):
         w = getattr(R, "w_" + name)
         wst[name, "x1"].wait_recv()
-        s = w.at[y, k, :, 0]
+        s = lambda: w.at[y, k, :, 0]
         wst[name, "y2"] = send(s, s, yside)
+        to_sibling(name, lambda: w.at[y, k, :, 0, a_])
         wst[name, "y1"].wait_recv()
-        s = w.at[:, k, :, 1, ah]
+        s = lambda: w.at[:, k, :, 1, ah]
         wst[name, "x2"] = send(s, s, xside)
+        to_sibling(name, lambda: w.at[y_, k, :, 1, ah])
 
     def w_3(name):
         w = getattr(R, "w_" + name)
         wst[name, "y2"].wait_recv()
+        to_sibling(name, lambda: w.at[y_, k, :, 0])
         wst[name, "x2"].wait_recv()
-        s = w.at[:, k]
-        wst[name, "core"] = send(s, s, core)
+        to_sibling(name, lambda: w.at[:, k, :, 1, a_])
 
     def w_4(name):
-        wst[name, "core"].wait_recv()
+        for cp in wst[name, "core"]:
+            cp.wait_recv()
 
     gst = {}
-
-    def add_into(dst, other, lead):
-        for_index = [()]
-        for n in lead:
-            for_index = [ix + (i,) for ix in for_index for i in range(n)]
-        for ix in for_index:
-            dst[ix] = (dst[ix].astype(f32) + other(ix).astype(f32)).astype(bf16)
 
     def g_0(name):
         g, b0 = getattr(R, "g_" + name), getattr(R, "b0_" + name)
-        gst[name, "core"] = send(g.at[:, 1 - k], b0, core)
+        gst[name, "core"] = send(lambda: g.at[:, k_], b0, core)
 
     def g_1(name):
         g, b0, b1 = getattr(R, "g_" + name), getattr(R, "b0_" + name), getattr(R, "b1_" + name)
-        gst[name, "core"].wait_recv()
+        if name != "qkv":
+            gst[name, "core"].wait_recv()
 
         def one(i):
             yy, cc = i // 4, i % 4
@@ -225,10 +249,10 @@
         loop(8, one)
         if use_x:
             b2 = getattr(R, "b2_" + name)
-            gst[name, "y1"] = send(b0.at[1 - y, :, 0], b1, yside)
-            gst[name, "x1"] = send(b0.at[:, :, 1, 1 - ah], b2, xside)
+            gst[name, "y1"] = send(lambda: b0.at[y_, :, 0], b1, yside)
+            gst[name, "x1"] = send(lambda: b0.at[:, :, 1, a_], b2, xside)
         else:
-            gst[name, "y1"] = send(b0.at[1 - y], b1, yside)
+            gst[name, "y1"] = send(lambda: b0.at[y_], b1, yside)
 
     def g_2(name):
         b0, b1 = getattr(R, "b0_" + name), getattr(R, "b1_" + name)
@@ -243,14 +267,14 @@
         def one(cc):
             b1[cc] = (b1[cc].astype(f32) + b0[y, cc, 0].astype(f32)).astype(bf16)
         loop(4, one)
-        gst[name, "x2"] = send(b1.at[:, 1 - ah], b3, xside)
+        gst[name, "x2"] = send(lambda: b1.at[:, a_], b3, xside)
         gst[name, "x1"].wait_recv()
 
         def two(i):
             yy, cc = i // 4, i % 4
             b2[yy, cc] = (b2[yy, cc].astype(f32) + b0[yy, cc, 1, ah].astype(f32)).astype(bf16)
         loop(8, two)
-        gst[name, "y2"] = send(b2.at[1 - y], b4, yside)
+        gst[name, "y2"] = send(lambda: b2.at[y_], b4, yside)
 
     def g_3(name):
         b1, z, b5 = (getattr(R, "%s_%s" % (i, name)) for i in ("b1", "z" if use_x else "b1", "b5"))
@@ -263,7 +287,7 @@
                 z[cc, 0] = (b1[cc, ah].astype(f32) + b3[cc].astype(f32)).astype(bf16)
                 z[cc, 1] = (b2[y, cc].astype(f32) + b4[cc].astype(f32)).astype(bf16)
             loop(4, one)
-        gst[name, "z"] = [send(z.at[(c + i) % 4], b5.at[i - 1], (a, r, (c + i) % 4)) for i in range(1, 4)]
+        gst[name, "z"] = [send(lambda cc=cc: z.at[cc], lambda i=i: b5.at[i], (a, r, cc)) for i, cc in enumerate(others)]
 
     def g_4(name):
         z, b5, fin = (getattr(R, "%s_%s" % (i, name)) for i in ("z" if use_x else "b1", "b5", "fin"))
@@ -275,7 +299,7 @@
                 for i in range(3):
                     total = total + b5[i, t].astype(f32)
                 fin[t, ah] = total.astype(bf16)
-            s = fin.at[:, ah]
+            s = lambda: fin.at[:, ah]
             gst[name, "x3"] = send(s, s, xside)
         else:
             for t in range(2):
@@ -286,11 +310,10 @@
                     fin[t, i2] = total.astype(bf16)
 
     def g_5(name):
-        fin = getattr(R, "fin_" + name)
         if use_x:
             gst[name, "x3"].wait_recv()
         rows, cols = BLOCK[name]
-        return fin[...].reshape(rows, cols).astype(f32)
+        getattr(R, name + "_o")[...] = getattr(R, "fin_" + name)[...].reshape(rows, cols)
 
     def weight(name, rr):
         w = getattr(R, "w_" + name)
@@ -301,14 +324,20 @@
     vec_cp = [send(R.vec, R.vecs.at[c], (a, r, (c + i) % 4)) for i in range(1, 4)]
     vec_cp += [send(R.vec, R.vecr.at[r], dev) for dev in (core, yside, diag)]
     w_z("qkv")
-    tok_sends, tok_wait = rows_in(R.tok, R.xo, 0)
     for cp in local[1:]:
         cp.wait()
     w_z("og")
+    w_z("up")
+    tok_sends, tok_wait = rows_in(R.tok, R.xo, 0)
+    w_z("d0")
     w_1("qkv")
-    w_z("up")
+    w_1("og")
     w_2("qkv")
-    w_z("dg")
+    w_1("up")
+    w_2("og")
+    w_3("qkv")
+    w_2("up")
+    w_3("og")
     for cp in vec_cp:
         cp.wait_recv()
 
@@ -336,17 +365,18 @@
     here = [R.xn.at[pl.ds(lo_row, 128), :], R.xn.at[pl.ds(hi_row, 128), :]]
     to_z = [send(s, s, zside) for s in here]
     to_core = [send(s, s, core) for s in here]
-    w_3("qkv")
-    w_1("og")
-    w_2("og")
+    w_z("d1")
     cot_sends, cot_wait = rows_in(R.cot, R.co, 1)
+    w_3("up")
+    w_1("d0")
+    w_4("qkv")
+    w_2("d0")
     qz = q + 2 - 4 * (q // 2)
     for cp in to_z:
         cp.wait_recv()
     there = [R.xn.at[pl.ds(pl.multiple_of(qz * 128, 128), 128), :],
              R.xn.at[pl.ds(pl.multiple_of((7 - qz) * 128, 128), 128), :]]
     to_core += [send(s, s, core) for s in there]
-    w_4("qkv")
     for cp in to_core:
         cp.wait_recv()
 
@@ -355,9 +385,7 @@
         R.qp[p] = (dot(R.n1[...], w[:, 0:128], 1, 0).astype(bf16).astype(f32) * 0.125).astype(bf16)
         R.kv[p] = dot(R.xn[...], w[:, 128:384], 1, 0).astype(bf16)
     loop(4, qkv_pair)
-    w_3("og")
-    w_1("up")
-    w_1("dg")
+    w_1("d1")
 
     lane = lax.broadcasted_iota(jnp.int32, (T, 128), 1)
     key_at = lax.broadcasted_iota(jnp.int32, (512, 128), 0)
@@ -403,10 +431,18 @@
             inv = 1.0 / total
             R.li[p, h:h + 1, :] = inv
             R.att[p, 64 * h:64 * h + 64, :] = (o[64 * h:64 * h + 64] * inv).astype(bf16)
-    loop(4, attend_pair)
+    def attend_step(p):
+        attend_pair(p)
+
+        @pl.when(p == 0)
+        def _():
+            w_3("d0")
+
+        @pl.when(p == 1)
+        def _():
+            w_2("d1")
+    loop(4, attend_step)
     w_4("og")
-    w_2("up")
-    w_2("dg")
 
     def lanes(cc):
         return pl.ds(pl.multiple_of(cc * 128, 128), 128)
@@ -429,8 +465,6 @@
 
     standard, _ = norm_parts(midrows())
     R.n2[...] = (standard * vec_row(3) + vec_row(4)).astype(bf16)
-    w_3("up")
-    w_3("dg")
     w_4("up")
 
     def up_block(rr):
@@ -439,52 +473,66 @@
         R.hid[rr] = (pre * s).astype(bf16)
         R.slp[rr] = (s * (1.0 + pre * (1.0 - s))).astype(bf16)
     loop(4, up_block)
-    w_4("dg")
+    w_3("d1")
+    w_4("d0")
+    w_4("d1")
     cot_wait()
 
     def down_block(cc):
-        br = dot(R.hid[0], R.w_dg[0, 0, cc].reshape(512, 256), 1, 0)
-        for rr in range(1, 4):
-            br = br + dot(R.hid[rr], R.w_dg[rr // 2, rr % 2, cc].reshape(512, 256), 1, 0)
+        br = 0.0
+        for rr in range(4):
+            for j in range(2):
+                w = getattr(R, "w_d%d" % j)[rr // 2, rr % 2, cc].reshape(256, 256)
+                br = br + dot(R.hid[rr, :, 256 * j:256 * j + 256], w, 1, 0)
         ffn = br[:, 0:128] + R.vecs[cc, 5:6, :]
         gate = sigmoid(br[:, 128:256] + R.vecs[cc, 6:7, :])
         R.out[cc] = (R.mid[cc] + gate * ffn).astype(bf16)
         g = R.co[cc].astype(f32)
         gf = (g * gate).astype(bf16)
         gg = (g * ffn * gate * (1.0 - gate)).astype(bf16)
-        R.pair[cc, :, 0:128] = gf
-        R.pair[cc, :, 128:256] = gg
+        R.pair[:, wide(cc)] = cat([gf, gg])
         R.sv[5, pl.ds(cc, 1), :] = jnp.sum(gf.astype(f32), axis=0, keepdims=True)
         R.sv[6, pl.ds(cc, 1), :] = jnp.sum(gg.astype(f32), axis=0, keepdims=True)
     loop(4, down_block)
     out_sends, out_wait = rows_out(R.out, R.out_o, 2)
 
-    def grad_down(i):
-        rr, cc = i // 4, i % 4
-        R.g_dg[rr // 2, rr % 2, cc] = dot(R.hid[rr], R.pair[cc], 0, 0).astype(bf16).reshape(2, 2, 128, 256)
-    loop(16, grad_down)
-    g_0("dg")
+    def grad_down(j, kk):
+        for yy in range(2):
+            g = dot(R.hid[2 * yy + kk, :, 256 * j:256 * j + 256], R.pair[...], 0, 0).astype(bf16)
+            for cc in range(4):
+                getattr(R, "g_d%d" % j)[yy, kk, cc] = g[:, 256 * cc:256 * cc + 256].reshape(2, 2, 64, 256)
+    for j in range(2):
+        grad_down(j, 1 - k)
+        g_0("d%d" % j)
+        grad_down(j, k)
+    g_1("d0")
 
     def back_up(rr):
-        gh = dot(R.pair[0], R.w_dg[rr // 2, rr % 2, 0].reshape(512, 256), 1, 1)
-        for cc in range(1, 4):
-            gh = gh + dot(R.pair[cc], R.w_dg[rr // 2, rr % 2, cc].reshape(512, 256), 1, 1)
+        gh = 0.0
+        for cc in range(4):
+            w = [getattr(R, "w_d%d" % j)[rr // 2, rr % 2, cc].reshape(256, 256) for j in range(2)]
+            gh = gh + dot(R.pair[:, 256 * cc:256 * cc + 256], cat(w, 0), 1, 1)
         gp = (gh * R.slp[rr].astype(f32)).astype(bf16)
         R.slp[rr] = gp
         tot = jnp.sum(gp.astype(f32), axis=0, keepdims=True)
         for i in range(4):
             R.sv[8 + rr, i:i + 1, :] = tot[:, 128 * i:128 * i + 128]
     loop(4, back_up)
-    g_1("dg")
-
-    def grad_up(rr):
-        R.g_up[rr // 2, rr % 2] = dot(R.n2[...], R.slp[rr], 0, 0).astype(bf16).reshape(4, 2, 2, 32, 512)
-    loop(4, grad_up)
+    g_1("d1")
+
+    def grad_up(yy, kk):
+        g = dot(R.n2[...], R.slp[2 * yy + kk], 0, 0).astype(bf16)
+        R.g_up[yy, kk] = g.reshape(4, 2, 2, 32, 512)
+    grad_up(0, 1 - k)
+    grad_up(1, 1 - k)
     g_0("up")
+    grad_up(0, k)
+    grad_up(1, k)
 
     gn = dot(R.slp[0], weight("up", 0), 1, 1)
     for rr in range(1, 4):
         gn = gn + dot(R.slp[rr], weight("up", rr), 1, 1)
+    g_1("up")
 
     def norm_back(v, grad, gain_row, at):
         std, inv = norm_parts(v)
@@ -505,24 +553,24 @@
         gate = R.g1[cc]
         ga = (g_mid * gate).astype(bf16)
         gg = (g_mid * R.ao[cc] * gate * (1.0 - gate)).astype(bf16)
-        R.pair[cc, :, 0:128] = ga
-        R.pair[cc, :, 128:256] = gg
+        R.pair[:, 256 * cc:256 * cc + 256] = cat([ga, gg])
         R.sv[4, cc:cc + 1, :] = jnp.sum(gg.astype(f32), axis=0, keepdims=True)
-    g_1("up")
-
     def grad_out(cc):
-        R.g_og[:, :, cc] = dot(R.att[...].reshape(512, T), R.pair[cc], 1, 0).astype(bf16).reshape(2, 2, 2, 2, 32, 256)
+        R.g_og[:, :, cc] = dot(R.att[...].reshape(512, T), R.pair[:, wide(cc)], 1, 0).astype(bf16).reshape(2, 2, 2, 2, 32, 256)
     loop(4, grad_out)
     g_0("og")
-    g_2("dg")
-    do = dot(R.w_og[:, :, 0].reshape(512, 256), R.pair[0], 1, 1)
-    for cc in range(1, 4):
-        do = do + dot(R.w_og[:, :, cc].reshape(512, 256), R.pair[cc], 1, 1)
+    g_2("d0")
+    do = 0.0
+    for cc in range(4):
+        do = do + dot(R.w_og[:, :, cc].reshape(512, 256), R.pair[:, 256 * cc:256 * cc + 256], 1, 1)
     for cc in range(4):
         R.mid[cc] = do[:, 128 * cc:128 * cc + 128]
+    for i in range(2):
+        R.hid[i] = R.xn[512 * i:512 * i + 512, :].T
+    R.hid[2, :, 0:256] = R.xn[1024:1280, :].T
+    R.hid[3] = R.n1[...].T
     g_1("og")
-    g_2("up")
-    g_3("dg")
+    g_2("d1")
 
     row_of = lax.broadcasted_iota(jnp.int32, (128, T), 0)
 
@@ -559,10 +607,38 @@
         R.kv[p, :, 0:128] = (grads[0][0] + grads[1][0]).astype(bf16)
         R.kv[p, :, 128:256] = (grads[0][1] + grads[1][1]).astype(bf16)
         R.qp[p] = (cat(queries, 0) * 0.125).astype(bf16).T
-    loop(4, back_pair)
-    g_2("og")
-    g_3("up")
-    g_4("dg")
+        gk = dot(R.hid[0], R.kv[p, 0:512, :], 1, 0) + dot(R.hid[1], R.kv[p, 512:1024, :], 1, 0)
+        gk = gk + dot(R.hid[2, :, 0:256], R.kv[p, 1024:1280, :], 1, 0)
+        g = cat([dot(R.hid[3], R.qp[p], 1, 0), gk]).astype(bf16)
+        R.g_qkv[p // 2, p % 2] = g.reshape(4, 2, 2, 32, 384)
+
+    def qkv_copy(yy):
+        return pltpu.make_async_remote_copy(
+            src_ref=R.g_qkv.at[yy, 1 - k], dst_ref=R.b0_qkv.at[yy], send_sem=R.qsem.at[0, yy], recv_sem=R.qsem.at[1, yy],
+            device_id=core, device_id_type=MESH)
+
+    def back_step(p):
+        back_pair(p)
+
+        @pl.when(p % 2 != k)
+        def _():
+            qkv_copy(p // 2).start()
+
+        @pl.when(p == 0)
+        def _():
+            g_3("d0")
+
+        @pl.when(p == 1)
+        def _():
+            g_2("up")
+            g_3("d1")
+
+        @pl.when(p == 2)
+        def _():
+            g_4("d0")
+            g_2("og")
+            g_3("up")
+    loop(4, back_step)
 
     def back_rows(first, count):
         rows = pl.ds(first, count)
@@ -582,20 +658,16 @@
     for i, row in enumerate(chunk_rows(q3)):
         R.ex[1, 128 * i:128 * i + 128, :] = back_rows(row, 128).astype(bf16)
     part_core = send(R.ex, R.exr, core)
+    for yy in range(2):
+        qkv_copy(yy).wait_recv()
+    g_1("qkv")
     mine2 = [back_rows(row, 128) for row in chunk_rows(q2)]
     part_core.wait_recv()
     for i in range(2):
         R.ez[128 * i:128 * i + 128, :] = (mine2[i] + R.exr[1, 128 * i:128 * i + 128, :].astype(f32)).astype(bf16)
     part_z = send(R.ez, R.ezr, zside)
-
-    def grad_qkv(p):
-        g = cat([dot(R.n1[...], R.qp[p], 0, 0), dot(R.xn[...], R.kv[p], 0, 0)]).astype(bf16)
-        R.g_qkv[p // 2, p % 2] = g.reshape(4, 2, 2, 32, 384)
-    loop(4, grad_qkv)
-    g_0("qkv")
     g_3("og")
-    g_4("up")
-
+    g_4("d1")
     for row, n, at in ((lo_row, 128, 0), (hi_row, 128, 128), (1024, 256, 256)):
         own = back_rows(row, n)
         for cc in range(4):
@@ -606,58 +678,47 @@
         for cc in range(4):
             R.mid[cc] = R.mid[cc] + more[:, 128 * cc:128 * cc + 128]
     loop(4, add_queries)
-    g_1("qkv")
+    g_4("up")
     part_z.wait_recv()
     for cc in range(4):
         here = slice(128 * cc, 128 * cc + 128)
         R.mid[cc, 0:256, :] = R.mid[cc, 0:256, :] + (R.exr[0, :, here].astype(f32) + R.ezr[:, here].astype(f32))
     gx = norm_back(xrows(), midrows(), 0, 0)
+    R.sva[c] = R.sv[...]
+    sv_z = [send(R.sv, R.sva.at[c], (a, r, (c + i) % 4)) for i in range(1, 4)]
     for cc in range(4):
         R.ing[cc] = (R.gm[cc] + gx[:, 128 * cc:128 * cc + 128]).astype(bf16)
+    g_2("qkv")
+    g_4("og")
     ing_sends, ing_wait = rows_out(R.ing, R.ing_o, 3)
-    g_2("qkv")
+
+    for cp in sv_z:
+        cp.wait_recv()
+    R.sv2[...] = (R.sva[0] + R.sva[1]) + (R.sva[2] + R.sva[3])
+    slot = 4 * ah + r if use_x else r
+    R.svr[slot] = R.sv2[...]
+    sv_all = [send(R.sv2, R.svr.at[slot], dev) for dev in corners]
     g_3("qkv")
-
-    s1 = send(R.sv, R.svr.at[0], core)
-    s1.wait_recv()
-    R.sv2[...] = R.sv[...] + R.svr[0]
-    s2 = send(R.sv2, R.svr.at[1], yside)
-    g_4("og")
-    s2.wait_recv()
-    R.sv3[...] = R.sv2[...] + R.svr[1]
-    if use_x:
-        s3 = send(R.sv3, R.svr.at[2], xside)
-        g_4("qkv")
-        s3.wait_recv()
-        R.sv4[...] = R.sv3[...] + R.svr[2]
-    else:
-        g_4("qkv")
-        R.sv4[...] = R.sv3[...]
-    s4 = [send(R.sv4, R.svr.at[2 + i], (a, r, (c + i) % 4)) for i in range(1, 4)]
-
-    R.dg_o[...] = g_5("dg")
-    R.up_o[...] = g_5("up")
-    R.og_o[...] = g_5("og")
-    g = g_5("qkv")
-    R.qkv_o[...] = cat([g[:, (2 * j + h) * 64:(2 * j + h + 1) * 64] for h in range(2) for j in range(3)])
-    for cp in s4:
+    for name in ("d0", "d1", "up", "og"):
+        g_5(name)
+    for cp in sv_all:
         cp.wait_recv()
-    R.svr[2] = R.sv4[...]
+    total = R.svr[0]
+    for i in range(1, 8 if use_x else 4):
+        total = total + R.svr[i]
+    R.sv2t[...] = total
     R.small_o[...] = jnp.zeros((16, 128), f32)
-    order = [2 + lax.rem(c - cc + 4, 4) for cc in range(4)]
-
-    def total_of(i, j):
-        v = R.svr[order[0], i, pl.ds(j, 1), :]
-        for cc in range(1, 4):
-            v = v + R.svr[order[cc], i, pl.ds(j, 1), :]
-        return v
     for i in range(7):
-        R.small_o[i:i + 1, :] = total_of(i, c)
+        R.small_o[i:i + 1, :] = R.sv2t[i, pl.ds(c, 1), :]
     for i in range(4):
-        R.small_o[8 + i:9 + i, :] = total_of(8 + r, i)
+        R.small_o[8 + i:9 + i, :] = R.sv2t[8 + r, i:i + 1, :]
+    g_4("qkv")
+    g_5("qkv")
 
     out_wait()
     ing_wait()
+    for yy in range(2):
+        qkv_copy(yy).wait_send()
     for cp in pending:
         cp.wait_send()
     for sends in (tok_sends, cot_sends, out_sends, ing_sends):
@@ -667,17 +728,16 @@
 def body(use_x, tokens, cotangent, norm1_gain, norm1_bias, qkv_weight, out_weight, gate1_weight,
          gate1_bias, norm2_gain, norm2_bias, up_weight, up_bias, down_weight, down_bias,
          gate2_weight, gate2_bias):
-    vec = jnp.concatenate([norm1_gain, norm1_bias, gate1_bias, norm2_gain, norm2_bias, down_bias,
-                           gate2_bias, jnp.zeros_like(gate2_bias), up_bias,
-                           jnp.zeros((512,), bf16)]).astype(f32).reshape(16, 128)
     hbm = pl.BlockSpec(memory_space=pl.ANY)
     vmem = pl.BlockSpec(memory_space=pltpu.VMEM)
     ins = {"tok": tokens, "cot": cotangent, "i_qkv": qkv_weight, "i_out": out_weight, "i_gate1": gate1_weight,
-           "i_up": up_weight, "i_down": down_weight, "i_gate2": gate2_weight, "vec": vec}
-    outs = {"out_o": ((2048, 128), bf16, hbm), "ing_o": ((2048, 128), bf16, hbm),
-            "qkv_o": ((128, 384), f32, vmem), "og_o": ((128, 256), f32, vmem),
-            "up_o": ((128, 512), f32, vmem), "dg_o": ((512, 256), f32, vmem),
-            "small_o": ((16, 128), f32, vmem)}
+           "i_up": up_weight, "i_down": down_weight, "i_gate2": gate2_weight,
+           "norm1_gain": norm1_gain, "norm1_bias": norm1_bias, "gate1_bias": gate1_bias, "norm2_gain": norm2_gain,
+           "norm2_bias": norm2_bias, "down_bias": down_bias, "gate2_bias": gate2_bias, "up_bias": up_bias}
+    outs = {"out_o": ((2048, 128), bf16, hbm), "ing_o": ((2048, 128), bf16, hbm)}
+    for name in NAMES:
+        outs[name + "_o"] = (BLOCK[name], bf16, vmem)
+    outs["small_o"] = ((16, 128), f32, vmem)
     scr = {}
     for name in NAMES:
         rows, cols = BLOCK[name]
@@ -697,36 +757,63 @@
             scr["b5_" + name] = ((3, 2, 2, rq, cols), bf16)
         scr["fin_" + name] = ((2, 2, rq, cols), bf16)
     scr.update({
-        "qstage": ((128, 384), bf16), "vecs": ((4, 16, 128), f32), "vecr": ((4, 16, 128), f32),
+        "qstage": ((128, 384), bf16), "vec": ((16, 128), f32), "vecs": ((4, 16, 128), f32), "vecr": ((4, 16, 128), f32),
         "xo": ((4, T, 128), bf16), "co": ((4, T, 128), bf16), "n1": ((T, D), bf16),
         "xn": ((1280, D), bf16), "qp": ((4, T, 128), bf16), "kv": ((4, 1280, 256), bf16),
         "p1": ((8, 512, 512), bf16), "p2": ((8, 512, 384), bf16), "po": ((8, 128, 256), bf16),
         "li": ((4, 8, T), f32), "att": ((4, 128, T), bf16), "ao": ((4, T, 128), f32),
         "g1": ((4, T, 128), f32), "mid": ((4, T, 128), f32), "n2": ((T, D), bf16),
         "hid": ((4, T, 512), bf16), "slp": ((4, T, 512), bf16), "out": ((4, T, 128), bf16),
-        "pair": ((4, T, 256), bf16), "gm": ((4, T, 128), f32), "ing": ((4, T, 128), bf16),
+        "pair": ((T, 1024), bf16), "gm": ((4, T, 128), f32), "ing": ((4, T, 128), bf16),
         "ex": ((2, 256, D), bf16), "exr": ((2, 256, D), bf16), "ez": ((256, D), bf16), "ezr": ((256, D), bf16),
-        "sv": ((12, 8, 128), f32), "sv2": ((12, 8, 128), f32), "sv3": ((12, 8, 128), f32),
-        "sv4": ((12, 8, 128), f32), "svr": ((6, 12, 8, 128), f32),
+        "sv": ((12, 8, 128), f32), "sva": ((4, 12, 8, 128), f32), "sv2": ((12, 8, 128), f32),
+        "sv2t": ((12, 8, 128), f32), "svr": ((8, 12, 8, 128), f32),
     })
     shapes = [pltpu.VMEM(s, d) for s, d in scr.values()]
-    names_scr = tuple(scr) + ("ssem", "rsem", "issem", "irsem", "lsem")
-    n_sem = 104
+    names_scr = tuple(scr) + ("ssem", "rsem", "issem", "irsem", "lsem", "qsem")
+    n_sem = 160
     dma = pltpu.SemaphoreType.DMA
-    shapes += [dma((n_sem,)), dma((n_sem,)), dma((4, 4, 3)), dma((4, 4, 3)), dma((16,))]
+    shapes += [dma((n_sem,)), dma((n_sem,)), dma((4, 4, 3)), dma((4, 4, 3)), dma((20,)), dma((2, 2))]
     res = pl.pallas_call(
         partial(kernel, use_x, tuple(ins), tuple(outs), names_scr),
         out_shape=[jax.ShapeDtypeStruct(s, d) for s, d, _ in outs.values()],
-        in_specs=[hbm] * 8 + [vmem],
+        in_specs=[hbm] * 8 + [vmem] * 8,
         out_specs=[sp for _, _, sp in outs.values()],
         scratch_shapes=shapes,
         compiler_params=pltpu.CompilerParams(collective_id=0, has_side_effects=True, vmem_limit_bytes=60 * 1024 * 1024),
     )(*ins.values())
-    output, input_grad, gq, gog, gup, gdg, small = res
     if not use_x:
-        gq, gog, gup, gdg, small = lax.psum((gq, gog, gup, gdg, small), "grp")
-    return (output, input_grad, small[0], small[1], gq, gog[:, :128], gog[:, 128:], small[4], small[2],
-            small[3], gup, small[8:12].reshape(512), gdg[:, :128], small[5], gdg[:, 128:], small[6])
+        summed = lax.psum(tuple(v.astype(f32) for v in res[2:]), "grp")
+        res = list(res[:2]) + list(summed)
+    flat = {"out": (2048, 128), "ing": (2048, 128), "n1g": (128,), "n1b": (128,), "qkv": (128, 384),
+            "w_out": (128, 128), "w_gate1": (128, 128), "g1b": (128,), "n2g": (128,), "n2b": (128,),
+            "up": (128, 512), "upb": (512,), "w_down": (512, 128), "db": (128,), "w_gate2": (512, 128), "g2b": (128,)}
+    kinds = {name: bf16 if name in ("out", "ing") else f32 for name in flat}
+    return pl.pallas_call(
+        finish,
+        out_shape=[jax.ShapeDtypeStruct(shape, kinds[name]) for name, shape in flat.items()],
+        in_specs=[vmem] * 8,
+        out_specs=[vmem] * 16,
+    )(*res)
+
+
+def finish(out_i, ing_i, qkv_i, og_i, up_i, d0_i, d1_i, small_i, out, ing, n1g, n1b, qkv, w_out, w_gate1, g1b, n2g, n2b,
+           up, upb, w_down, db, w_gate2, g2b):
+    out[...] = out_i[...]
+    ing[...] = ing_i[...]
+    g = qkv_i[...].astype(f32)
+    qkv[...] = cat([g[:, (2 * j + h) * 64:(2 * j + h + 1) * 64] for h in range(2) for j in range(3)])
+    w_out[...] = og_i[:, 0:128].astype(f32)
+    w_gate1[...] = og_i[:, 128:256].astype(f32)
+    up[...] = up_i[...].astype(f32)
+    w_down[0:256, :] = d0_i[:, 0:128].astype(f32)
+    w_down[256:512, :] = d1_i[:, 0:128].astype(f32)
+    w_gate2[0:256, :] = d0_i[:, 128:256].astype(f32)
+    w_gate2[256:512, :] = d1_i[:, 128:256].astype(f32)
+    for i, ref in enumerate((n1g, n1b, n2g, n2b, g1b, db, g2b)):
+        ref[...] = small_i[i:i + 1, :].reshape(128)
+    for i in range(4):
+        upb[128 * i:128 * i + 128] = small_i[8 + i:9 + i, :].reshape(128)
 
 
 def solution(mesh):

time: 190 us -> 155 us (0.82)
  Pallas kernels: 173 us -> 154 us
  local copies, waits for them, and re-layouts: 15.1 us -> 0 us
    pallas_call x1, Pallas kernels: 173 us -> 151 us  [body(): pl.pallas_call(partial(kernel, use_x, tuple(ins), tuple(outs), names_scr)...]
    unnamed x39 -> x0, local copies, waits for them, and re-layouts: 10.4 us -> none
    slice x2 -> x0, local copies, waits for them, and re-layouts: 3.44 us -> none  [the longest x1 1.91 us: body(): gdg[:, 128:]]
    pallas_call x0 -> x1, Pallas kernels: none -> 2.78 us  [body(): pl.pallas_call(finish, out_shape=[jax.ShapeDtypeStruct(shape, kinds[name]...]
where the time goes in v2:
time: 155 us; the launch traced here: 154 us
  Pallas kernels  154 us (99%)
    pallas_call x1, Pallas kernels, body(): pl.pallas_call(partial(kernel, use_x, tuple(ins), tuple(outs), names_scr)...  151 us

profile of v2, /device:TPU:0, one launch (start us, length us, event | category | flops | bytes accessed | tf_op | source)
XLA Modules:
  0.0 154.4 jit_solution(13015554506009091195)
XLA Ops:
  0.7 150.8 %shard_map.279 = (bf16[2048,128]{1,0:T(8,128)(2,1)}, bf16[2048,128]{1,0:T(8,128)(2,1)}, bf16[128,384]{1,0:T(8,128)(2,1)}, bf16[128,256]{1,0:T(8,128)(2,1)}, bf16...) custom-call(bf16[2048,128]{1,0:T(8,128)(2,1)} %refs_0_.1, ...), custom_call_target="tpu_custom_call" | custom-call | tf_op jit(solution)/shard_map/pallas_call | solution.py:777
  151.5 2.8 %shard_map.280 = (bf16[2048,128]{1,0:T(8,128)(2,1)}, bf16[2048,128]{1,0:T(8,128)(2,1)}, f32[128]{0:T(128)}, f32[128]{0:T(128)}, f32[128,384]{1,0:T(8,128)}, /*in...) custom-call(bf16[2048,128]{1,0:T(8,128)(2,1)} %get-tuple-element.24., ...), custom_call_target="tpu_custom_call" | custom-call | tf_op jit(solution)/shard_map/pallas_call | solution.py:792

commit v3 on v2

--- a/solution.py
+++ b/solution.py
@@ -57,6 +57,9 @@
     ah = a % 2
     q = 2 * (c % 2) + k
     y_, k_, a_ = 1 - y, 1 - k, 1 - ah
+    c_far = lax.rem(c + 2, 4)
+    c_near = c + 1 - 2 * (c % 2)
+    c_across = lax.rem(c_near + 2, 4)
     others = [lax.rem(c + i, 4) for i in range(1, 4)]
     core = (a, 2 * y + 1 - k, c)
     yside = (a, 2 * (1 - y) + k, c)
@@ -156,11 +159,13 @@
                     pltpu.make_async_copy(d, d, R.irsem.at[which, cc, j]).wait()
         return sends, wait
 
-    def rows_out(src, dst, which):
+    def rows_out(src, dst, which, only=(0, 1, 2)):
         sends = []
         for cc in range(4):
             me = (c // 2 == k) & (c == cc)
             for j, (s0, d0, n) in enumerate(((0, lo_row, 128), (128, hi_row, 128), (256, 1024 + pl.multiple_of(q * 256, 256), 256))):
+                if j not in only:
+                    continue
                 s = src.at[cc, pl.ds(s0, n), :]
                 d = dst.at[pl.ds(d0, n), :]
                 rs = R.irsem.at[which, q, j]
@@ -195,15 +200,22 @@
     def w_z(name):
         w = getattr(R, "w_" + name)
         here = lambda: w.at[y, k, c, :, ah]
-        wst[name, "z"] = [send(here, here, (a, r, cc)) for cc in others]
+        wst[name, "far"] = send(here, here, (a, r, c_far))
+        wst[name, "near"] = send(here, here, zside)
+
+    def w_f(name):
+        w = getattr(R, "w_" + name)
+        wst[name, "far"].wait_recv()
+        here = lambda: w.at[y, k, c_far, :, ah]
+        wst[name, "on"] = send(here, here, zside)
 
     def to_sibling(name, s):
         wst.setdefault((name, "core"), []).append(send(s, s, core))
 
     def w_1(name):
         w = getattr(R, "w_" + name)
-        for cp in wst[name, "z"]:
-            cp.wait_recv()
+        wst[name, "near"].wait_recv()
+        wst[name, "on"].wait_recv()
         s = lambda: w.at[y, k, :, 0, ah]
         wst[name, "x1"] = send(s, s, xside)
         s = lambda: w.at[y, k, :, 1, ah]
@@ -287,29 +299,28 @@
                 z[cc, 0] = (b1[cc, ah].astype(f32) + b3[cc].astype(f32)).astype(bf16)
                 z[cc, 1] = (b2[y, cc].astype(f32) + b4[cc].astype(f32)).astype(bf16)
             loop(4, one)
-        gst[name, "z"] = [send(lambda cc=cc: z.at[cc], lambda i=i: b5.at[i], (a, r, cc)) for i, cc in enumerate(others)]
+        gst[name, "near"] = [send(lambda cc=cc: z.at[cc], lambda i=i: b5.at[i], zside) for i, cc in enumerate((c_near, c_across))]
 
     def g_4(name):
-        z, b5, fin = (getattr(R, "%s_%s" % (i, name)) for i in ("z" if use_x else "b1", "b5", "fin"))
-        for cp in gst[name, "z"]:
+        z, b5, b6 = (getattr(R, "%s_%s" % (i, name)) for i in ("z" if use_x else "b1", "b5", "b6"))
+        for cp in gst[name, "near"]:
             cp.wait_recv()
+        b5[1] = (b5[1].astype(f32) + z[c_far].astype(f32)).astype(bf16)
+        gst[name, "far"] = send(lambda: b5.at[1], b6, (a, r, c_far))
+
+    def g_5(name):
+        z, b5, b6, fin = (getattr(R, "%s_%s" % (i, name)) for i in ("z" if use_x else "b1", "b5", "b6", "fin"))
+        gst[name, "far"].wait_recv()
+        total = z[c].astype(f32) + b5[0].astype(f32) + b6[...].astype(f32)
         if use_x:
             for t in range(2):
-                total = z[c, t].astype(f32)
-                for i in range(3):
-                    total = total + b5[i, t].astype(f32)
-                fin[t, ah] = total.astype(bf16)
+                fin[t, ah] = total[t].astype(bf16)
             s = lambda: fin.at[:, ah]
             gst[name, "x3"] = send(s, s, xside)
         else:
-            for t in range(2):
-                for i2 in range(2):
-                    total = z[c, t, i2].astype(f32)
-                    for i in range(3):
-                        total = total + b5[i, t, i2].astype(f32)
-                    fin[t, i2] = total.astype(bf16)
-
-    def g_5(name):
+            fin[...] = total.astype(bf16)
+
+    def g_6(name):
         if use_x:
             gst[name, "x3"].wait_recv()
         rows, cols = BLOCK[name]
@@ -327,17 +338,21 @@
     for cp in local[1:]:
         cp.wait()
     w_z("og")
+    w_f("qkv")
     w_z("up")
-    tok_sends, tok_wait = rows_in(R.tok, R.xo, 0)
+    w_f("og")
+    w_1("qkv")
     w_z("d0")
-    w_1("qkv")
     w_1("og")
+    w_f("up")
     w_2("qkv")
     w_1("up")
+    w_f("d0")
+    tok_sends, tok_wait = rows_in(R.tok, R.xo, 0)
     w_2("og")
+    w_1("d0")
     w_3("qkv")
     w_2("up")
-    w_3("og")
     for cp in vec_cp:
         cp.wait_recv()
 
@@ -366,11 +381,10 @@
     to_z = [send(s, s, zside) for s in here]
     to_core = [send(s, s, core) for s in here]
     w_z("d1")
-    cot_sends, cot_wait = rows_in(R.cot, R.co, 1)
+    w_3("og")
+    w_2("d0")
+    w_4("qkv")
     w_3("up")
-    w_1("d0")
-    w_4("qkv")
-    w_2("d0")
     qz = q + 2 - 4 * (q // 2)
     for cp in to_z:
         cp.wait_recv()
@@ -385,7 +399,8 @@
         R.qp[p] = (dot(R.n1[...], w[:, 0:128], 1, 0).astype(bf16).astype(f32) * 0.125).astype(bf16)
         R.kv[p] = dot(R.xn[...], w[:, 128:384], 1, 0).astype(bf16)
     loop(4, qkv_pair)
-    w_1("d1")
+    w_f("d1")
+    cot_sends, cot_wait = rows_in(R.cot, R.co, 1)
 
     lane = lax.broadcasted_iota(jnp.int32, (T, 128), 1)
     key_at = lax.broadcasted_iota(jnp.int32, (512, 128), 0)
@@ -436,9 +451,10 @@
 
         @pl.when(p == 0)
         def _():
+            w_1("d1")
             w_3("d0")
 
-        @pl.when(p == 1)
+        @pl.when(p == 2)
         def _():
             w_2("d1")
     loop(4, attend_step)
@@ -532,21 +548,23 @@
     gn = dot(R.slp[0], weight("up", 0), 1, 1)
     for rr in range(1, 4):
         gn = gn + dot(R.slp[rr], weight("up", rr), 1, 1)
-    g_1("up")
-
-    def norm_back(v, grad, gain_row, at):
+
+    def norm_back(v, grad, gain_row):
         std, inv = norm_parts(v)
         gs = jnp.sum(grad * std, axis=0, keepdims=True)
         gb = jnp.sum(grad, axis=0, keepdims=True)
+        s = grad * vec_row(gain_row)
+        f = jnp.sum(s, axis=1, keepdims=True) * (1.0 / D)
+        e = jnp.sum(s * std, axis=1, keepdims=True) * (1.0 / D)
+        return inv * (s - f - std * e), gs, gb
+
+    def put_sums(at, gs, gb):
         for cc in range(4):
             R.sv[at, cc:cc + 1, :] = gs[:, 128 * cc:128 * cc + 128]
             R.sv[at + 1, cc:cc + 1, :] = gb[:, 128 * cc:128 * cc + 128]
-        s = grad * vec_row(gain_row)
-        f = jnp.sum(s, axis=1, keepdims=True) * (1.0 / D)
-        e = jnp.sum(s * std, axis=1, keepdims=True) * (1.0 / D)
-        return inv * (s - f - std * e)
-
-    gm = norm_back(midrows(), gn, 3, 2)
+
+    gm, gs, gb = norm_back(midrows(), gn, 3)
+    put_sums(2, gs, gb)
     for cc in range(4):
         g_mid = R.co[cc].astype(f32) + gm[:, 128 * cc:128 * cc + 128]
         R.gm[cc] = g_mid
@@ -555,11 +573,13 @@
         gg = (g_mid * R.ao[cc] * gate * (1.0 - gate)).astype(bf16)
         R.pair[:, 256 * cc:256 * cc + 256] = cat([ga, gg])
         R.sv[4, cc:cc + 1, :] = jnp.sum(gg.astype(f32), axis=0, keepdims=True)
+    g_2("d0")
+    g_1("up")
+
     def grad_out(cc):
         R.g_og[:, :, cc] = dot(R.att[...].reshape(512, T), R.pair[:, wide(cc)], 1, 0).astype(bf16).reshape(2, 2, 2, 2, 32, 256)
     loop(4, grad_out)
     g_0("og")
-    g_2("d0")
     do = 0.0
     for cc in range(4):
         do = do + dot(R.w_og[:, :, cc].reshape(512, 256), R.pair[:, 256 * cc:256 * cc + 256], 1, 1)
@@ -570,7 +590,6 @@
     R.hid[2, :, 0:256] = R.xn[1024:1280, :].T
     R.hid[3] = R.n1[...].T
     g_1("og")
-    g_2("d1")
 
     row_of = lax.broadcasted_iota(jnp.int32, (128, T), 0)
 
@@ -626,19 +645,14 @@
 
         @pl.when(p == 0)
         def _():
-            g_3("d0")
+            g_2("d1")
 
         @pl.when(p == 1)
         def _():
-            g_2("up")
-            g_3("d1")
-
-        @pl.when(p == 2)
-        def _():
-            g_4("d0")
-            g_2("og")
-            g_3("up")
+            g_3("d0")
     loop(4, back_step)
+    g_2("up")
+    g_4("d0")
 
     def back_rows(first, count):
         rows = pl.ds(first, count)
@@ -660,15 +674,18 @@
     part_core = send(R.ex, R.exr, core)
     for yy in range(2):
         qkv_copy(yy).wait_recv()
+    g_2("og")
     g_1("qkv")
     mine2 = [back_rows(row, 128) for row in chunk_rows(q2)]
     part_core.wait_recv()
     for i in range(2):
         R.ez[128 * i:128 * i + 128, :] = (mine2[i] + R.exr[1, 128 * i:128 * i + 128, :].astype(f32)).astype(bf16)
     part_z = send(R.ez, R.ezr, zside)
-    g_3("og")
-    g_4("d1")
-    for row, n, at in ((lo_row, 128, 0), (hi_row, 128, 128), (1024, 256, 256)):
+
+    def x_rows(at, n):
+        return cat([R.xo[cc, at:at + n, :] for cc in range(4)]).astype(f32)
+
+    def own_rows(row, n, at):
         own = back_rows(row, n)
         for cc in range(4):
             R.mid[cc, at:at + n, :] = own[:, 128 * cc:128 * cc + 128]
@@ -677,20 +694,35 @@
         more = dot(R.qp[p], weight("qkv", p)[:, 0:128], 1, 1)
         for cc in range(4):
             R.mid[cc] = R.mid[cc] + more[:, 128 * cc:128 * cc + 128]
+
+    def to_input(at, n):
+        gx, gs, gb = norm_back(x_rows(at, n), cat([R.mid[cc, at:at + n, :] for cc in range(4)]), 0)
+        for cc in range(4):
+            R.ing[cc, at:at + n, :] = (R.gm[cc, at:at + n, :] + gx[:, 128 * cc:128 * cc + 128]).astype(bf16)
+        return gs, gb
+
+    own_rows(lo_row, 128, 0)
+    own_rows(hi_row, 128, 128)
+    own_rows(1024, 256, 256)
     loop(4, add_queries)
-    g_4("up")
+    g_3("d1")
+    gs2, gb2 = to_input(256, 256)
+    g_3("up")
+    ing_sends2, _ = rows_out(R.ing, R.ing_o, 3, (2,))
+    g_5("d0")
+    g_3("og")
+    g_4("d1")
     part_z.wait_recv()
     for cc in range(4):
         here = slice(128 * cc, 128 * cc + 128)
         R.mid[cc, 0:256, :] = R.mid[cc, 0:256, :] + (R.exr[0, :, here].astype(f32) + R.ezr[:, here].astype(f32))
-    gx = norm_back(xrows(), midrows(), 0, 0)
+    gs, gb = to_input(0, 256)
+    put_sums(0, gs + gs2, gb + gb2)
     R.sva[c] = R.sv[...]
     sv_z = [send(R.sv, R.sva.at[c], (a, r, (c + i) % 4)) for i in range(1, 4)]
-    for cc in range(4):
-        R.ing[cc] = (R.gm[cc] + gx[:, 128 * cc:128 * cc + 128]).astype(bf16)
+    ing_sends, ing_wait = rows_out(R.ing, R.ing_o, 3, (0, 1))
     g_2("qkv")
-    g_4("og")
-    ing_sends, ing_wait = rows_out(R.ing, R.ing_o, 3)
+    g_4("up")
 
     for cp in sv_z:
         cp.wait_recv()
@@ -698,9 +730,12 @@
     slot = 4 * ah + r if use_x else r
     R.svr[slot] = R.sv2[...]
     sv_all = [send(R.sv2, R.svr.at[slot], dev) for dev in corners]
+    g_5("d1")
+    g_4("og")
     g_3("qkv")
-    for name in ("d0", "d1", "up", "og"):
-        g_5(name)
+    g_5("up")
+    g_5("og")
+    g_4("qkv")
     for cp in sv_all:
         cp.wait_recv()
     total = R.svr[0]
@@ -712,8 +747,9 @@
         R.small_o[i:i + 1, :] = R.sv2t[i, pl.ds(c, 1), :]
     for i in range(4):
         R.small_o[8 + i:9 + i, :] = R.sv2t[8 + r, i:i + 1, :]
-    g_4("qkv")
     g_5("qkv")
+    for name in NAMES:
+        g_6(name)
 
     out_wait()
     ing_wait()
@@ -721,7 +757,7 @@
         qkv_copy(yy).wait_send()
     for cp in pending:
         cp.wait_send()
-    for sends in (tok_sends, cot_sends, out_sends, ing_sends):
+    for sends in (tok_sends, cot_sends, out_sends, ing_sends2, ing_sends):
         finish_sends(sends)
 
 
@@ -751,10 +787,12 @@
             scr["b3_" + name] = ((4, rq, cols), bf16)
             scr["b4_" + name] = ((4, rq, cols), bf16)
             scr["z_" + name] = ((4, 2, rq, cols), bf16)
-            scr["b5_" + name] = ((3, 2, rq, cols), bf16)
+            scr["b5_" + name] = ((2, 2, rq, cols), bf16)
+            scr["b6_" + name] = ((2, rq, cols), bf16)
         else:
             scr["b1_" + name] = ((4, 2, 2, rq, cols), bf16)
-            scr["b5_" + name] = ((3, 2, 2, rq, cols), bf16)
+            scr["b5_" + name] = ((2, 2, 2, rq, cols), bf16)
+            scr["b6_" + name] = ((2, 2, rq, cols), bf16)
         scr["fin_" + name] = ((2, 2, rq, cols), bf16)
     scr.update({
         "qstage": ((128, 384), bf16), "vec": ((16, 128), f32), "vecs": ((4, 16, 128), f32), "vecr": ((4, 16, 128), f32),

time: 155 us -> 147 us (0.948)
  Pallas kernels: 154 us -> 146 us
    pallas_call x1, Pallas kernels: 151 us -> 143 us  [body(): pl.pallas_call(partial(kernel, use_x, tuple(ins), tuple(outs), names_scr)...]
where the time goes in v3:
time: 147 us
  Pallas kernels  146 us (99%)
    pallas_call x1, Pallas kernels, body(): pl.pallas_call(partial(kernel, use_x, tuple(ins), tuple(outs), names_scr)...  143 us

profile of v3, /device:TPU:0, one launch (start us, length us, event | category | flops | bytes accessed | tf_op | source)
XLA Modules:
  0.0 146.5 jit_solution(6872157405098556071)
XLA Ops:
  0.7 143.0 %shard_map.279 = (bf16[2048,128]{1,0:T(8,128)(2,1)}, bf16[2048,128]{1,0:T(8,128)(2,1)}, bf16[128,384]{1,0:T(8,128)(2,1)}, bf16[128,256]{1,0:T(8,128)(2,1)}, bf16...) custom-call(bf16[2048,128]{1,0:T(8,128)(2,1)} %refs_0_.1, ...), custom_call_target="tpu_custom_call" | custom-call | tf_op jit(solution)/shard_map/pallas_call | solution.py:815
  143.6 2.8 %shard_map.280 = (bf16[2048,128]{1,0:T(8,128)(2,1)}, bf16[2048,128]{1,0:T(8,128)(2,1)}, f32[128]{0:T(128)}, f32[128]{0:T(128)}, f32[128,384]{1,0:T(8,128)}, /*in...) custom-call(bf16[2048,128]{1,0:T(8,128)(2,1)} %get-tuple-element.24., ...), custom_call_target="tpu_custom_call" | custom-call | tf_op jit(solution)/shard_map/pallas_call | solution.py:830

commit v4 on v3

--- a/solution.py
+++ b/solution.py
@@ -60,6 +60,7 @@
     c_far = lax.rem(c + 2, 4)
     c_near = c + 1 - 2 * (c % 2)
     c_across = lax.rem(c_near + 2, 4)
+    slot = 4 * ah + r if use_x else r
     others = [lax.rem(c + i, 4) for i in range(1, 4)]
     core = (a, 2 * y + 1 - k, c)
     yside = (a, 2 * (1 - y) + k, c)
@@ -124,6 +125,7 @@
         parts = [blk[:, (3 * h + j) * 64:(3 * h + j + 1) * 64] for j in range(3) for h in range(2)]
         R.w_qkv[y, k, c, t, ah] = cat(parts).astype(bf16)
     R.vec[...] = jnp.zeros((16, 128), f32)
+    R.svb[32:40, :] = jnp.zeros((8, 128), f32)
     for i, name in enumerate(VECTORS):
         R.vec[i:i + 1, :] = getattr(R, name)[...].astype(f32).reshape(1, 128)
     for i in range(4):
@@ -391,6 +393,7 @@
     there = [R.xn.at[pl.ds(pl.multiple_of(qz * 128, 128), 128), :],
              R.xn.at[pl.ds(pl.multiple_of((7 - qz) * 128, 128), 128), :]]
     to_core += [send(s, s, core) for s in there]
+    w_f("d1")
     for cp in to_core:
         cp.wait_recv()
 
@@ -399,8 +402,8 @@
         R.qp[p] = (dot(R.n1[...], w[:, 0:128], 1, 0).astype(bf16).astype(f32) * 0.125).astype(bf16)
         R.kv[p] = dot(R.xn[...], w[:, 128:384], 1, 0).astype(bf16)
     loop(4, qkv_pair)
-    w_f("d1")
     cot_sends, cot_wait = rows_in(R.cot, R.co, 1)
+    w_1("d1")
 
     lane = lax.broadcasted_iota(jnp.int32, (T, 128), 1)
     key_at = lax.broadcasted_iota(jnp.int32, (512, 128), 0)
@@ -451,10 +454,9 @@
 
         @pl.when(p == 0)
         def _():
-            w_1("d1")
             w_3("d0")
 
-        @pl.when(p == 2)
+        @pl.when(p == 1)
         def _():
             w_2("d1")
     loop(4, attend_step)
@@ -507,8 +509,8 @@
         gf = (g * gate).astype(bf16)
         gg = (g * ffn * gate * (1.0 - gate)).astype(bf16)
         R.pair[:, wide(cc)] = cat([gf, gg])
-        R.sv[5, pl.ds(cc, 1), :] = jnp.sum(gf.astype(f32), axis=0, keepdims=True)
-        R.sv[6, pl.ds(cc, 1), :] = jnp.sum(gg.astype(f32), axis=0, keepdims=True)
+        R.svb[pl.ds(12 + cc, 1), :] = jnp.sum(gf.astype(f32), axis=0, keepdims=True)
+        R.svb[pl.ds(16 + cc, 1), :] = jnp.sum(gg.astype(f32), axis=0, keepdims=True)
     loop(4, down_block)
     out_sends, out_wait = rows_out(R.out, R.out_o, 2)
 
@@ -532,7 +534,7 @@
         R.slp[rr] = gp
         tot = jnp.sum(gp.astype(f32), axis=0, keepdims=True)
         for i in range(4):
-            R.sv[8 + rr, i:i + 1, :] = tot[:, 128 * i:128 * i + 128]
+            R.svb[pl.ds(20 + 4 * rr + i, 1), :] = tot[:, 128 * i:128 * i + 128]
     loop(4, back_up)
     g_1("d1")
 
@@ -558,13 +560,32 @@
         e = jnp.sum(s * std, axis=1, keepdims=True) * (1.0 / D)
         return inv * (s - f - std * e), gs, gb
 
-    def put_sums(at, gs, gb):
+    def put_sums(to, gs, gb):
         for cc in range(4):
-            R.sv[at, cc:cc + 1, :] = gs[:, 128 * cc:128 * cc + 128]
-            R.sv[at + 1, cc:cc + 1, :] = gb[:, 128 * cc:128 * cc + 128]
+            to[cc:cc + 1, :] = gs[:, 128 * cc:128 * cc + 128]
+            to[4 + cc:5 + cc, :] = gb[:, 128 * cc:128 * cc + 128]
+
+    def small_1(v, parts):
+        parts[c] = v[...]
+        return [send(v, lambda: parts.at[c], (a, r, cc)) for cc in others]
+
+    def small_2(sent, parts, mine, alls):
+        for cp in sent:
+            cp.wait_recv()
+        mine[...] = (parts[0] + parts[1]) + (parts[2] + parts[3])
+        alls[slot] = mine[...]
+        return [send(mine, lambda: alls.at[slot], dev) for dev in corners]
+
+    def small_3(sent, alls, total):
+        for cp in sent:
+            cp.wait_recv()
+        v = alls[0]
+        for i in range(1, 8 if use_x else 4):
+            v = v + alls[i]
+        total[...] = v
 
     gm, gs, gb = norm_back(midrows(), gn, 3)
-    put_sums(2, gs, gb)
+    put_sums(R.svb, gs, gb)
     for cc in range(4):
         g_mid = R.co[cc].astype(f32) + gm[:, 128 * cc:128 * cc + 128]
         R.gm[cc] = g_mid
@@ -572,7 +593,7 @@
         ga = (g_mid * gate).astype(bf16)
         gg = (g_mid * R.ao[cc] * gate * (1.0 - gate)).astype(bf16)
         R.pair[:, 256 * cc:256 * cc + 256] = cat([ga, gg])
-        R.sv[4, cc:cc + 1, :] = jnp.sum(gg.astype(f32), axis=0, keepdims=True)
+        R.svb[8 + cc:9 + cc, :] = jnp.sum(gg.astype(f32), axis=0, keepdims=True)
     g_2("d0")
     g_1("up")
 
@@ -590,6 +611,7 @@
     R.hid[2, :, 0:256] = R.xn[1024:1280, :].T
     R.hid[3] = R.n1[...].T
     g_1("og")
+    svb_1 = small_1(R.svb, R.svb_parts)
 
     row_of = lax.broadcasted_iota(jnp.int32, (128, T), 0)
 
@@ -676,6 +698,7 @@
         qkv_copy(yy).wait_recv()
     g_2("og")
     g_1("qkv")
+    svb_2 = small_2(svb_1, R.svb_parts, R.svb_mine, R.svb_all)
     mine2 = [back_rows(row, 128) for row in chunk_rows(q2)]
     part_core.wait_recv()
     for i in range(2):
@@ -717,36 +740,28 @@
         here = slice(128 * cc, 128 * cc + 128)
         R.mid[cc, 0:256, :] = R.mid[cc, 0:256, :] + (R.exr[0, :, here].astype(f32) + R.ezr[:, here].astype(f32))
     gs, gb = to_input(0, 256)
-    put_sums(0, gs + gs2, gb + gb2)
-    R.sva[c] = R.sv[...]
-    sv_z = [send(R.sv, R.sva.at[c], (a, r, (c + i) % 4)) for i in range(1, 4)]
+    put_sums(R.sva, gs + gs2, gb + gb2)
+    sva_1 = small_1(R.sva, R.sva_parts)
     ing_sends, ing_wait = rows_out(R.ing, R.ing_o, 3, (0, 1))
     g_2("qkv")
     g_4("up")
 
-    for cp in sv_z:
-        cp.wait_recv()
-    R.sv2[...] = (R.sva[0] + R.sva[1]) + (R.sva[2] + R.sva[3])
-    slot = 4 * ah + r if use_x else r
-    R.svr[slot] = R.sv2[...]
-    sv_all = [send(R.sv2, R.svr.at[slot], dev) for dev in corners]
+    sva_2 = small_2(sva_1, R.sva_parts, R.sva_mine, R.sva_all)
     g_5("d1")
     g_4("og")
     g_3("qkv")
     g_5("up")
     g_5("og")
     g_4("qkv")
-    for cp in sv_all:
-        cp.wait_recv()
-    total = R.svr[0]
-    for i in range(1, 8 if use_x else 4):
-        total = total + R.svr[i]
-    R.sv2t[...] = total
+    small_3(svb_2, R.svb_all, R.svb_total)
+    small_3(sva_2, R.sva_all, R.sva_total)
     R.small_o[...] = jnp.zeros((16, 128), f32)
-    for i in range(7):
-        R.small_o[i:i + 1, :] = R.sv2t[i, pl.ds(c, 1), :]
+    for i in range(2):
+        R.small_o[i:i + 1, :] = R.sva_total[pl.ds(4 * i + c, 1), :]
+    for i in range(5):
+        R.small_o[2 + i:3 + i, :] = R.svb_total[pl.ds(4 * i + c, 1), :]
     for i in range(4):
-        R.small_o[8 + i:9 + i, :] = R.sv2t[8 + r, i:i + 1, :]
+        R.small_o[8 + i:9 + i, :] = R.svb_total[pl.ds(20 + 4 * r + i, 1), :]
     g_5("qkv")
     for name in NAMES:
         g_6(name)
@@ -804,8 +819,8 @@
         "hid": ((4, T, 512), bf16), "slp": ((4, T, 512), bf16), "out": ((4, T, 128), bf16),
         "pair": ((T, 1024), bf16), "gm": ((4, T, 128), f32), "ing": ((4, T, 128), bf16),
         "ex": ((2, 256, D), bf16), "exr": ((2, 256, D), bf16), "ez": ((256, D), bf16), "ezr": ((256, D), bf16),
-        "sv": ((12, 8, 128), f32), "sva": ((4, 12, 8, 128), f32), "sv2": ((12, 8, 128), f32),
-        "sv2t": ((12, 8, 128), f32), "svr": ((8, 12, 8, 128), f32),
+        "sva": ((8, 128), f32), "sva_parts": ((4, 8, 128), f32), "sva_mine": ((8, 128), f32), "sva_total": ((8, 128), f32), "sva_all": ((8, 8, 128), f32),
+        "svb": ((40, 128), f32), "svb_parts": ((4, 40, 128), f32), "svb_mine": ((40, 128), f32), "svb_total": ((40, 128), f32), "svb_all": ((8, 40, 128), f32),
     })
     shapes = [pltpu.VMEM(s, d) for s, d in scr.values()]
     names_scr = tuple(scr) + ("ssem", "rsem", "issem", "irsem", "lsem", "qsem")

time: 147 us -> 142 us (0.966)
  Pallas kernels: 146 us -> 141 us
    pallas_call x1, Pallas kernels: 143 us -> 139 us  [body(): pl.pallas_call(partial(kernel, use_x, tuple(ins), tuple(outs), names_scr)...]
where the time goes in v4:
time: 142 us
  Pallas kernels  141 us (99%)
    pallas_call x1, Pallas kernels, body(): pl.pallas_call(partial(kernel, use_x, tuple(ins), tuple(outs), names_scr)...  139 us

profile of v4, /device:TPU:0, one launch (start us, length us, event | category | flops | bytes accessed | tf_op | source)
XLA Modules:
  0.0 142.1 jit_solution(6099130407287932863)
XLA Ops:
  0.7 138.6 %shard_map.279 = (bf16[2048,128]{1,0:T(8,128)(2,1)}, bf16[2048,128]{1,0:T(8,128)(2,1)}, bf16[128,384]{1,0:T(8,128)(2,1)}, bf16[128,256]{1,0:T(8,128)(2,1)}, bf16...) custom-call(bf16[2048,128]{1,0:T(8,128)(2,1)} %refs_0_.1, ...), custom_call_target="tpu_custom_call" | custom-call | tf_op jit(solution)/shard_map/pallas_call | solution.py:830
  139.2 2.8 %shard_map.280 = (bf16[2048,128]{1,0:T(8,128)(2,1)}, bf16[2048,128]{1,0:T(8,128)(2,1)}, f32[128]{0:T(128)}, f32[128]{0:T(128)}, f32[128,384]{1,0:T(8,128)}, /*in...) custom-call(bf16[2048,128]{1,0:T(8,128)(2,1)} %get-tuple-element.24., ...), custom_call_target="tpu_custom_call" | custom-call | tf_op jit(solution)/shard_map/pallas_call | solution.py:845

commit v5 on v4

--- a/solution.py
+++ b/solution.py
@@ -696,14 +696,14 @@
     part_core = send(R.ex, R.exr, core)
     for yy in range(2):
         qkv_copy(yy).wait_recv()
-    g_2("og")
-    g_1("qkv")
-    svb_2 = small_2(svb_1, R.svb_parts, R.svb_mine, R.svb_all)
     mine2 = [back_rows(row, 128) for row in chunk_rows(q2)]
     part_core.wait_recv()
     for i in range(2):
         R.ez[128 * i:128 * i + 128, :] = (mine2[i] + R.exr[1, 128 * i:128 * i + 128, :].astype(f32)).astype(bf16)
     part_z = send(R.ez, R.ezr, zside)
+    g_2("og")
+    g_1("qkv")
+    svb_2 = small_2(svb_1, R.svb_parts, R.svb_mine, R.svb_all)
 
     def x_rows(at, n):
         return cat([R.xo[cc, at:at + n, :] for cc in range(4)]).astype(f32)

time: 142 us -> 141 us (level)
  no operation moved by 1% of the time
where the time goes in v5:
time: 141 us
  Pallas kernels  140 us (99%)
    pallas_call x1, Pallas kernels, body(): pl.pallas_call(partial(kernel, use_x, tuple(ins), tuple(outs), names_scr)...  138 us

profile of v5, /device:TPU:0, one launch (start us, length us, event | category | flops | bytes accessed | tf_op | source)
XLA Modules:
  0.0 141.2 jit_solution(9401913057066077488)
XLA Ops:
  0.7 137.7 %shard_map.279 = (bf16[2048,128]{1,0:T(8,128)(2,1)}, bf16[2048,128]{1,0:T(8,128)(2,1)}, bf16[128,384]{1,0:T(8,128)(2,1)}, bf16[128,256]{1,0:T(8,128)(2,1)}, bf16...) custom-call(bf16[2048,128]{1,0:T(8,128)(2,1)} %refs_0_.1, ...), custom_call_target="tpu_custom_call" | custom-call | tf_op jit(solution)/shard_map/pallas_call | solution.py:830
  138.3 2.8 %shard_map.280 = (bf16[2048,128]{1,0:T(8,128)(2,1)}, bf16[2048,128]{1,0:T(8,128)(2,1)}, f32[128]{0:T(128)}, f32[128]{0:T(128)}, f32[128,384]{1,0:T(8,128)}, /*in...) custom-call(bf16[2048,128]{1,0:T(8,128)(2,1)} %get-tuple-element.24., ...), custom_call_target="tpu_custom_call" | custom-call | tf_op jit(solution)/shard_map/pallas_call | solution.py:845

commit v6 on v5

--- a/solution.py
+++ b/solution.py
@@ -732,7 +732,6 @@
     gs2, gb2 = to_input(256, 256)
     g_3("up")
     ing_sends2, _ = rows_out(R.ing, R.ing_o, 3, (2,))
-    g_5("d0")
     g_3("og")
     g_4("d1")
     part_z.wait_recv()
@@ -744,6 +743,7 @@
     sva_1 = small_1(R.sva, R.sva_parts)
     ing_sends, ing_wait = rows_out(R.ing, R.ing_o, 3, (0, 1))
     g_2("qkv")
+    g_5("d0")
     g_4("up")
 
     sva_2 = small_2(sva_1, R.sva_parts, R.sva_mine, R.sva_all)

time: 141 us -> 141 us (level)
  no operation moved by 1% of the time
where the time goes in v6:
time: 141 us
  Pallas kernels  140 us (99%)
    pallas_call x1, Pallas kernels, body(): pl.pallas_call(partial(kernel, use_x, tuple(ins), tuple(outs), names_scr)...  138 us

profile of v6, /device:TPU:0, one launch (start us, length us, event | category | flops | bytes accessed | tf_op | source)
XLA Modules:
  0.0 141.2 jit_solution(13359056118520312909)
XLA Ops:
  0.7 137.7 %shard_map.279 = (bf16[2048,128]{1,0:T(8,128)(2,1)}, bf16[2048,128]{1,0:T(8,128)(2,1)}, bf16[128,384]{1,0:T(8,128)(2,1)}, bf16[128,256]{1,0:T(8,128)(2,1)}, bf16...) custom-call(bf16[2048,128]{1,0:T(8,128)(2,1)} %refs_0_.1, ...), custom_call_target="tpu_custom_call" | custom-call | tf_op jit(solution)/shard_map/pallas_call | solution.py:830
  138.3 2.8 %shard_map.280 = (bf16[2048,128]{1,0:T(8,128)(2,1)}, bf16[2048,128]{1,0:T(8,128)(2,1)}, f32[128]{0:T(128)}, f32[128]{0:T(128)}, f32[128,384]{1,0:T(8,128)}, /*in...) custom-call(bf16[2048,128]{1,0:T(8,128)(2,1)} %get-tuple-element.24., ...), custom_call_target="tpu_custom_call" | custom-call | tf_op jit(solution)/shard_map/pallas_call | solution.py:845
